TPU v7x, 256 devices: a whole 4x4x8 slice. The times are simulated.
256 devices in a mesh: outer: 64 (over y_lo, z, x), inner: 4 (over y_hi, core).
Axes of the slice: x: 4, y: 4 (y_hi: 2, y_lo: 2; y = y_hi * 2 + y_lo), z: 8, core: 2. Of those that a mesh axis runs over, the one named last changes fastest.
Arguments:
- frames: bfloat16 [32768, 1024], P(('outer', 'inner')), may hold values from -6 to 6
- gain_attn: float32 [1024], replicated, may hold values from 0.5 to 2
- w_query: bfloat16 [1024, 512], replicated, may hold values from -4 to 4
- w_key: bfloat16 [1024, 512], replicated, may hold values from -0.1875 to 0.1875
- w_value: bfloat16 [1024, 512], replicated, may hold values from -0.1875 to 0.1875
- w_out: bfloat16 [512, 1024], replicated, may hold values from -0.25 to 0.25
- gain_conv: float32 [1024], replicated, may hold values from 0.5 to 2
- w_expand: bfloat16 [1024, 2048], replicated, may hold values from -0.1875 to 0.1875
- kernel_taps: float32 [31, 1024], replicated, may hold values from -2 to 2
- bn_scale: float32 [1024], replicated, may hold values from 0.5 to 2
- bn_shift: float32 [1024], replicated, may hold values from -3 to 3
- w_project: bfloat16 [1024, 1024], replicated, may hold values from -0.1875 to 0.1875
Outputs:
- block_out: bfloat16 [32768, 1024], P(('outer', 'inner'))
All inputs are finite; a program needn't handle non-finite values.
Results may differ from a plain program's by a relative error of at most 0.017.
The roundings to bfloat16 on the way count: a program that leaves them out, or rounds other values in their place, can miss the bound.
Values may be sent and summed in bfloat16 or wider, within the bound.
No kernel may reach another device: no remote copies, remote signals or barrier semaphores. Data moves between devices by JAX's collectives and lax.ppermute only.
A program may use at most 128 MiB of HBM per device.

v0:
```python
import jax
import jax.numpy as jnp
from jax import lax
from jax.sharding import PartitionSpec as P

HEAD_DIM = 64


def with_halo(cells, sides, width):
    for axis, dim in sides:
        count = lax.axis_size(axis)
        ends = count - 1
        head = lax.slice_in_dim(cells, 0, width, axis=dim)
        tail = lax.slice_in_dim(cells, cells.shape[dim] - width, cells.shape[dim], axis=dim)
        cells = jnp.concatenate(
            [
                lax.ppermute(tail, axis, [(i, (i + 1) % count) for i in range(ends)]),
                cells,
                lax.ppermute(head, axis, [((i + 1) % count, i) for i in range(ends)]),
            ],
            axis=dim,
        )
    return cells


def norm_rows(values, gain):
    values = values.astype(jnp.float32)
    center = values - jnp.mean(values, axis=-1, keepdims=True)
    spread = jnp.mean(center * center, axis=-1, keepdims=True)
    return center * lax.rsqrt(spread + 1e-05) * gain


def attend_update(carry, query_heads, key_piece, value_piece, scale):
    rows = key_piece.shape[0]
    head_count = query_heads.shape[1]
    head_size = query_heads.shape[2]
    block = 512
    key_blocks = key_piece.reshape(rows // block, block, head_count, head_size)
    value_blocks = value_piece.reshape(rows // block, block, head_count, head_size)

    def one_block(state, pair):
        accum, top, total = state
        key_block, value_block = pair
        scores = (
            jnp.einsum("qhd,khd->qhk", query_heads, key_block, preferred_element_type=jnp.float32)
            * scale
        )
        new_top = jnp.maximum(top, jnp.max(scores, axis=-1))
        factor = jnp.exp(top - new_top)
        weights = jnp.exp(scores - new_top[:, :, None])
        total = total * factor + jnp.sum(weights, axis=-1)
        mixed = jnp.einsum(
            "qhk,khd->qhd",
            weights.astype(jnp.bfloat16),
            value_block,
            preferred_element_type=jnp.float32,
        )
        accum = accum * factor[:, :, None] + mixed
        return ((accum, new_top, total), None)

    carry, unused = lax.scan(one_block, carry, (key_blocks, value_blocks))
    return carry


def body(
    frames,
    gain_attn,
    w_query,
    w_key,
    w_value,
    w_out,
    gain_conv,
    w_expand,
    kernel_taps,
    bn_scale,
    bn_shift,
    w_project,
):
    own_rows = frames.shape[0]
    model_width = frames.shape[1]
    group = lax.axis_size("inner")
    head_size = HEAD_DIM
    width = w_query.shape[1]
    local_width = width // group
    local_heads = local_width // head_size
    scale = head_size ** (-0.5)
    normed = norm_rows(frames, gain_attn).astype(jnp.bfloat16)
    start_col = lax.axis_index("inner") * local_width
    chosen = jnp.concatenate(
        [
            lax.dynamic_slice_in_dim(w_query, start_col, local_width, 1),
            lax.dynamic_slice_in_dim(w_key, start_col, local_width, 1),
            lax.dynamic_slice_in_dim(w_value, start_col, local_width, 1),
        ],
        axis=1,
    )
    projected = jnp.dot(
        lax.all_gather(normed, "inner", axis=0, tiled=True),
        chosen,
        preferred_element_type=jnp.float32,
    ).astype(jnp.bfloat16)
    query_local = projected[:, :local_width]
    key_local = projected[:, local_width : 2 * local_width]
    value_local = projected[:, 2 * local_width :]
    block_rows = group * own_rows
    query_heads = query_local.reshape(block_rows, local_heads, head_size)
    start_state = (
        jnp.zeros((block_rows, local_heads, head_size), jnp.float32),
        jnp.full((block_rows, local_heads), -jnp.inf, jnp.float32),
        jnp.zeros((block_rows, local_heads), jnp.float32),
    )
    final_state = attend_update(
        start_state,
        query_heads,
        lax.all_gather(key_local, "outer", axis=0, tiled=True),
        lax.all_gather(value_local, "outer", axis=0, tiled=True),
        scale,
    )
    accum, top, total = final_state
    context_local = (
        (accum / total[:, :, None]).astype(jnp.bfloat16).reshape(block_rows, 1, local_width)
    )
    returned = lax.all_to_all(context_local, "inner", split_axis=0, concat_axis=1, tiled=True)
    context = returned.reshape(own_rows, width)
    attn = jnp.dot(context, w_out, preferred_element_type=jnp.float32)
    hidden = (frames.astype(jnp.float32) + attn).astype(jnp.bfloat16)
    normed2 = norm_rows(hidden, gain_conv).astype(jnp.bfloat16)
    expand = jnp.dot(normed2, w_expand, preferred_element_type=jnp.float32)
    glu = (expand[:, :model_width] * jax.nn.sigmoid(expand[:, model_width:])).astype(jnp.bfloat16)
    taps = kernel_taps.shape[0]
    half_kernel = taps // 2
    padded = with_halo(glu, ((("outer", "inner"), 0),), half_kernel)
    conv = jnp.zeros((own_rows, model_width), jnp.float32)
    for tap in range(taps):
        conv = conv + kernel_taps[tap] * padded[tap : tap + own_rows].astype(jnp.float32)
    act = jax.nn.silu(bn_scale * conv + bn_shift).astype(jnp.bfloat16)
    result = hidden.astype(jnp.float32) + jnp.dot(
        act, w_project, preferred_element_type=jnp.float32
    )
    return result.astype(jnp.bfloat16)


def solution(mesh):
    return jax.shard_map(
        body,
        mesh=mesh,
        in_specs=(
            P(("outer", "inner"), None),
            P(),
            P(),
            P(),
            P(),
            P(),
            P(),
            P(),
            P(),
            P(),
            P(),
            P(),
        ),
        out_specs=P(("outer", "inner"), None),
        check_vma=False,
    )
```

profile of v0, /device:TPU:1, one launch (start us, length us, event | category | flops | bytes accessed | tf_op | source)
XLA Modules:
  0.0 1131.6 jit_solution(17595431488501985609)
XLA Ops:
  13.0 25.6 %all-gather.4.cloned.1.call-done = bf16[512,1024]{1,0:T(8,128)(2,1)} async-done(((bf16[128,1024]{1,0:T(8,128)(2,1)}), bf16[512,1024]{1,0:T(8,128)(2,1)}) %all-gather.4.cloned.1.call-update) | async-done | bytes 1048592 | tf_op jit(solution)/shard_map/all_gather | solution.py:98
  41.9 269.5 %all-gather.6.cloned.1.call-done = bf16[32768,128]{0,1:T(8,128)(2,1)} async-done(((bf16[512,128]{0,1:T(8,128)(2,1)}), bf16[32768,128]{0,1:T(8,128)(2,1)}) %all-gather.6.cloned.1.call-update) | async-done | bytes 8388624 | tf_op jit(solution)/shard_map/all_gather | solution.py:115
  311.4 10.1 copy.36
  321.6 11.3 %copy.30 = bf16[64,512,2,64]{1,3,2,0:T(8,128)(2,1)} copy(bf16[64,512,2,64]{1,0,3,2:T(8,128)(2,1)} %bitcast.89) | data formatting | bytes 16777216
  332.9 289.6 %all-gather.8.cloned.1.call-done = bf16[32768,128]{0,1:T(8,128)(2,1)} async-done(((bf16[512,128]{0,1:T(8,128)(2,1)}), bf16[32768,128]{0,1:T(8,128)(2,1)}) %all-gather.8.cloned.1.call-update) | async-done | bytes 8388624 | tf_op jit(solution)/shard_map/all_gather | solution.py:116
  622.5 10.3 copy.37
  632.8 11.4 %copy.31 = bf16[64,512,2,64]{1,3,2,0:T(8,128)(2,1)} copy(bf16[64,512,2,64]{1,0,3,2:T(8,128)(2,1)} %bitcast.90) | data formatting | bytes 16777216
  644.2 409.9 %while.15 = (s32[]{:T(128)}, f32[512,2,64]{0,2,1:T(8,128)S(1)}, f32[512,2]{0,1:T(2,128)S(1)}, f32[512,2]{0,1:T(2,128)S(1)}, bf16[64,512,2,64]{1,3,2,0:T(8,128)(2...) while((s32[]{:T(128)}, f32[512,2,64]{0,2,1:T(8,128)S(1)}, ...), condition=%wide.region_5.6_spmd.clone, body=%wide.region_2.5_spmd.clone.sunk | while | flops 138613760 | bytes 15664261 | solution.py:61
  644.2 2.8 bitcast_reduce_fusion.2
  650.6 2.7 bitcast_reduce_fusion.2
  663.4 2.7 bitcast_reduce_fusion.2
  676.2 2.7 bitcast_reduce_fusion.2
  689.0 2.7 bitcast_reduce_fusion.2
  701.9 2.7 bitcast_reduce_fusion.2
  714.7 2.7 bitcast_reduce_fusion.2
  727.5 2.7 bitcast_reduce_fusion.2
  740.3 2.7 bitcast_reduce_fusion.2
  753.1 2.7 bitcast_reduce_fusion.2
  765.9 2.7 bitcast_reduce_fusion.2
  778.7 2.7 bitcast_reduce_fusion.2
  791.5 2.7 bitcast_reduce_fusion.2
  804.3 2.7 bitcast_reduce_fusion.2
  810.7 2.7 bitcast_reduce_fusion.2
  817.1 2.7 bitcast_reduce_fusion.2
  829.9 2.7 bitcast_reduce_fusion.2
  842.8 2.7 bitcast_reduce_fusion.2
  855.6 2.7 bitcast_reduce_fusion.2
  868.4 2.7 bitcast_reduce_fusion.2
  881.2 2.7 bitcast_reduce_fusion.2
  894.0 2.7 bitcast_reduce_fusion.2
  906.8 2.7 bitcast_reduce_fusion.2
  919.6 2.7 bitcast_reduce_fusion.2
  932.4 2.7 bitcast_reduce_fusion.2
  945.2 2.7 bitcast_reduce_fusion.2
  958.0 2.7 bitcast_reduce_fusion.2
  970.8 2.7 bitcast_reduce_fusion.2
  983.6 2.7 bitcast_reduce_fusion.2
  996.5 2.7 bitcast_reduce_fusion.2
  1009.3 2.7 bitcast_reduce_fusion.2
  1022.1 2.7 bitcast_reduce_fusion.2
  1034.9 2.7 bitcast_reduce_fusion.2
  1047.7 2.7 bitcast_reduce_fusion.2
  1056.1 45.4 %all-to-all-start = ((bf16[4,2,8192]{2,1,0:T(2,128)(2,1)}), bf16[4,2,8192]{2,1,0:T(2,128)(2,1)S(1)}, u32[]{:S(2)}, u32[]{:S(2)}) async-start(bf16[4,2,8192]{2,1,0:T(2,128)(2,1)} %reshape.52), calls=%async_computation | async-start | bytes 262144 | tf_op jit(solution)/shard_map/all_to_all | solution.py:123
  1101.6 5.0 all-to-all-done
  1108.9 3.0 fusion.35
  1112.0 2.9 collective-permute-start
  1116.9 4.8 collective-permute-done.1
  1121.7 3.4 fusion.19
  (526 shorter events, 330.5 us)
Async XLA Ops:
  6.5 1115.1 %copy-start = (bf16[1024,1024]{1,0:T(8,128)(2,1)S(1)}, bf16[1024,1024]{1,0:T(8,128)(2,1)}, u32[]{:S(2)}) copy-start(bf16[1024,1024]{1,0:T(8,128)(2,1)} %param.25) | copy-start | bytes 6291460
  6.5 32.0 %all-gather.4.cloned.1.call-start = ((), (), s32[]{:S(2)}) async-start(), calls=%async_computation.1 | async-start | bytes 1310720 | tf_op jit(solution)/shard_map/all_gather | solution.py:98
  10.9 300.6 %all-gather.6.cloned.1.call-start = ((), (), s32[]{:S(2)}) async-start(), calls=%async_computation.2 | async-start | bytes 8519680 | tf_op jit(solution)/shard_map/all_gather | solution.py:115
  41.1 581.4 %all-gather.8.cloned.1.call-start = ((), (), s32[]{:S(2)}) async-start(), calls=%async_computation.3 | async-start | bytes 8519680 | tf_op jit(solution)/shard_map/all_gather | solution.py:116
  644.2 457.4 %copy-start.3 = (f32[31,1024]{1,0:T(8,128)S(1)}, f32[31,1024]{1,0:T(8,128)}, u32[]{:S(2)}) copy-start(f32[31,1024]{1,0:T(8,128)} %param.22) | copy-start | bytes 380932
  647.0 2.2 copy-start.1
  653.4 2.2 copy-start.1
  659.8 2.2 copy-start.1
  666.2 2.2 copy-start.1
  672.6 2.2 copy-start.1
  679.0 2.2 copy-start.1
  685.4 2.2 copy-start.1
  691.8 2.2 copy-start.1
  698.2 2.2 copy-start.1
  704.6 2.2 copy-start.1
  711.0 2.2 copy-start.1
  717.4 2.2 copy-start.1
  723.8 2.2 copy-start.1
  730.2 2.2 copy-start.1
  743.0 2.2 copy-start.1
  749.4 2.2 copy-start.1
  755.8 2.2 copy-start.1
  762.2 2.2 copy-start.1
  768.6 2.2 copy-start.1
  775.0 2.2 copy-start.1
  787.8 2.2 copy-start.1
  794.3 2.2 copy-start.1
  800.7 2.2 copy-start.1
  807.1 2.2 copy-start.1
  813.5 2.2 copy-start.1
  819.9 2.2 copy-start.1
  826.3 2.2 copy-start.1
  832.7 2.2 copy-start.1
  839.1 2.2 copy-start.1
  845.5 2.2 copy-start.1
  851.9 2.2 copy-start.1
  858.3 2.2 copy-start.1
  864.7 2.2 copy-start.1
  871.1 2.2 copy-start.1
  877.5 2.2 copy-start.1
  883.9 2.2 copy-start.1
  1054.1 52.9 %copy-start.2 = (bf16[128,1024]{1,0:T(8,128)(2,1)S(1)}, bf16[128,1024]{1,0:T(8,128)(2,1)}, u32[]{:S(2)}) copy-start(bf16[128,1024]{1,0:T(8,128)(2,1)} %param.14) | copy-start | bytes 786436
  1055.4 53.4 %copy-start.4 = (f32[1024]{0:T(1024)S(1)}, f32[1024]{0:T(1024)}, u32[]{:S(2)}) copy-start(f32[1024]{0:T(1024)} %param.20) | copy-start | bytes 12292
  1056.1 50.5 %all-to-all-start = ((bf16[4,2,8192]{2,1,0:T(2,128)(2,1)}), bf16[4,2,8192]{2,1,0:T(2,128)(2,1)S(1)}, u32[]{:S(2)}, u32[]{:S(2)}) async-start(bf16[4,2,8192]{2,1,0:T(2,128)(2,1)} %reshape.52), calls=%async_computation | async-start | bytes 262144 | tf_op jit(solution)/shard_map/all_to_all | solution.py:123
  1108.8 12.8 %copy-start.5 = (f32[1024]{0:T(1024)S(1)}, f32[1024]{0:T(1024)}, u32[]{:S(2)}) copy-start(f32[1024]{0:T(1024)} %param.24) | copy-start | bytes 12292
  1108.9 12.8 %copy-start.6 = (f32[1024]{0:T(1024)S(1)}, f32[1024]{0:T(1024)}, u32[]{:S(2)}) copy-start(f32[1024]{0:T(1024)} %param.23) | copy-start | bytes 12292
  1112.0 4.9 collective-permute-start
  1114.9 6.7 collective-permute-start.1
  (28 other events, 62.2 us)
Sparse Core Ops, SparseCore 0:
  11.0 27.5 all-gather.3
  41.3 270.1 all-gather.5
  313.2 309.2 all-gather.7
where the time goes:
time: 1130 us
  waiting for transfers between devices  595 us (53%)
  matrix products  275 us (24%)
  other arithmetic  141 us (12%)
  local copies, waits for them, and re-layouts  53.5 us (5%)
  starting transfers between devices  50.3 us (4%)
  between operations  13.3 us (1%)
    all_gather x1, waiting for transfers between devices, body(): lax.all_gather(value_local, 'outer', axis=0, tiled=True)  290 us
    all_gather x1, waiting for transfers between devices, body(): lax.all_gather(key_local, 'outer', axis=0, tiled=True)  270 us
    dot_general x64, matrix products, one_block(): jnp.einsum('qhd,khd->qhk', query_heads, key_block, preferred_element_type...  175 us
    reduce_sum x64, other arithmetic, one_block(): total = total * factor + jnp.sum(weights, axis=-1)  134 us
    dot_general x64, matrix products, one_block(): jnp.einsum('qhk,khd->qhd', weights.astype(jnp.bfloat16), value_block, pre...  90.4 us
    all_to_all x1, starting transfers between devices, body(): lax.all_to_all(context_local, 'inner', split_axis=0, concat_axis=1, tiled...  45.4 us
    unnamed x20, local copies, waits for them, and re-layouts  44.1 us
    all_gather x1, waiting for transfers between devices, body(): lax.all_gather(normed, 'inner', axis=0, tiled=True)  25.6 us
  transfers between devices with their start and end apart: 6, of which 5 were waited for; matrix products, arithmetic and copies ran while one was open for 2% of the time, Pallas kernels for 0%

commit v1 on v0

v1 whole, which is shorter than its diff:
```python
import functools

import jax
import jax.numpy as jnp
from jax import lax
from jax.experimental import pallas as pl
from jax.experimental.pallas import tpu as pltpu
from jax.sharding import Mesh
from jax.sharding import PartitionSpec as P

BF = jnp.bfloat16
F32 = jnp.float32
D = 1024
HD = 64
OWN = 128
GRP = 1024
EPS = 1e-05
C = 0.125 * 1.4426950408889634
T_LOW, T_HIGH = 2.0 ** -60, 2.0 ** 100
TQ = 512
VMEM_LIMIT = 56 * 2 ** 20
NAMES = ("ylo", "z", "x", "yhi", "core")
YC = ("ylo", "yhi", "core")
VM = pl.BlockSpec(memory_space=pltpu.VMEM)
SM = pl.BlockSpec(memory_space=pltpu.SMEM)
ANY = pl.BlockSpec(memory_space=pl.ANY)


def call(kernel, ins, specs, outs, scratch=(), us=2):
    return pl.pallas_call(
        kernel,
        in_specs=specs,
        out_specs=[VM] * len(outs),
        out_shape=[jax.ShapeDtypeStruct(s, d) for s, d in outs],
        scratch_shapes=list(scratch),
        compiler_params=pltpu.CompilerParams(vmem_limit_bytes=VMEM_LIMIT),
        cost_estimate=pl.CostEstimate(flops=int(us * 1e9), bytes_accessed=1024, transcendentals=0),
    )(*ins)


def norm_rows(values, gain):
    values = values.astype(F32)
    center = values - jnp.mean(values, axis=-1, keepdims=True)
    spread = jnp.mean(center * center, axis=-1, keepdims=True)
    return center * lax.rsqrt(spread + EPS) * gain


def mm(a, b):
    return jnp.dot(a, b, preferred_element_type=F32)


def split3(row):
    hi = row.astype(BF)
    rest = row - hi.astype(F32)
    mid = rest.astype(BF)
    low = (rest - mid.astype(F32)).astype(BF)
    return hi, mid, low


def stats_rows(total, top):
    width = total.shape[1]
    index = lax.broadcasted_iota(jnp.int32, (16, width), 0)
    out = jnp.zeros((16, width), F32)
    for place, part in enumerate(split3(total) + split3(top)):
        out = jnp.where(index == place, jnp.broadcast_to(part.astype(F32), (16, width)), out)
    return out.astype(BF)


def stats_read(rows):
    rows = rows.astype(F32)
    return rows[0:1] + rows[1:2] + rows[2:3], rows[3:4] + rows[4:5] + rows[5:6]


def project_kernel(pos, own, sib, gain, wq, wk, wv, m0, m1, m2, m3, wbuf, sems):
    y, core = pos[0], pos[1]
    cols = pl.ds(pl.multiple_of(core * 256, 256), 256)
    copies = [
        pltpu.make_async_copy(w.at[:, cols], wbuf.at[i], sems.at[i]) for i, w in enumerate((wk, wv, wq))
    ]
    for copy in copies:
        copy.start()
    g = gain[...]
    normed = jnp.concatenate(
        [norm_rows(own[...], g).astype(BF), norm_rows(sib[...], g).astype(BF)], axis=0
    )
    copies[0].wait()
    k = mm(normed, wbuf[0])
    copies[1].wait()
    vt = mm(normed, wbuf[1]).T.astype(BF)
    copies[2].wait()
    qt = mm(normed, wbuf[2]).T.astype(BF)
    blocks = []
    for h in range(4):
        pair = jnp.concatenate([k[:OWN, h * HD:(h + 1) * HD], k[OWN:, h * HD:(h + 1) * HD]], axis=1).astype(BF)
        vh, qh = vt[h * HD:(h + 1) * HD], qt[h * HD:(h + 1) * HD]
        blocks.append(jnp.concatenate([pair, vh[:, :OWN], vh[:, OWN:], qh[:, :OWN], qh[:, OWN:]], axis=0))
    outs = (m0, m1, m2, m3)
    for here in range(4):
        @pl.when(y == here)
        def _():
            for i in range(4):
                outs[i][...] = blocks[(here + i) % 4]


def pair_and_values(kv, half):
    lhs = kv[0:512, :]
    cols = jnp.concatenate([kv[512 + half * 256 + i * 64:512 + half * 256 + (i + 1) * 64, :] for i in range(4)], axis=1)
    return lhs, jnp.concatenate([jnp.ones((64, 512), BF), cols], axis=0)


def place(q, half):
    zero = jnp.zeros((64, q.shape[1]), BF)
    return jnp.concatenate([q, zero] if half == 0 else [zero, q], axis=0)


def pack_kernel(a0, a1, a2, a3, kv, qx):
    parts = (a0, a1, a2, a3)
    for i, a in enumerate(parts):
        kv[i * 128:(i + 1) * 128, :] = a[0:128, :]
        kv[512 + i * 64:512 + (i + 1) * 64, :] = a[128:192, :]
        kv[768 + i * 64:768 + (i + 1) * 64, :] = a[192:256, :]
        qx[0:64, (2 * i) * 128:(2 * i + 1) * 128] = a[256:320, :]
        qx[0:64, (2 * i + 1) * 128:(2 * i + 2) * 128] = a[320:384, :]
    s = mm(kv[0:512, :], place(qx[0:64, :], 0))
    top = jnp.max(s, axis=0, keepdims=True)
    qx[64:80, :] = stats_rows(jnp.zeros_like(top), top)


def augmented(q, stats):
    unused, top = stats_read(stats)
    shift = top.astype(BF)
    width = shift.shape[1]
    index = lax.broadcasted_iota(jnp.int32, (128, width), 0)
    bias = jnp.where(index == 0, jnp.broadcast_to(-shift.astype(F32), (128, width)), 0.0).astype(BF)
    return [jnp.concatenate([place(q, half), bias], axis=0) for half in (0, 1)], shift.astype(F32)


def one_column(rows):
    lane = lax.broadcasted_iota(jnp.int32, (rows, 128), 1)
    return jnp.where(lane == 0, 1.0, 0.0).astype(BF)


def attend(rhs, chunks, acc):
    ones = one_column(512)

    def weights(step):
        kv, half = chunks[step // 2], step % 2
        lhs, values = pair_and_values(kv, half)
        s = mm(jnp.concatenate([lhs, ones], axis=1), rhs[half])
        return jnp.exp2(s * C).astype(BF), values

    steps = 2 * len(chunks)
    now = weights(0)
    for step in range(steps):
        later = weights(step + 1) if step + 1 < steps else None
        acc = acc + mm(now[1], now[0])
        now = later
    return acc


def exact(q_ref, chunks, kv_s, acc_ref, top_ref):
    for i, ref in enumerate(chunks):
        pltpu.sync_copy(ref, kv_s.at[i])

    def tile(t, carry):
        cols = pl.ds(pl.multiple_of(t * 256, 256), 256)
        q = q_ref[0:64, cols]

        def chunk(i, state):
            acc, old = state
            kv = kv_s.at[i]
            for half in (0, 1):
                lhs, values = pair_and_values(kv, half)
                s = mm(lhs, place(q, half))
                new = jnp.maximum(old, jnp.max(s, axis=0, keepdims=True))
                p = jnp.exp2((s - new) * C).astype(BF)
                acc = acc * jnp.exp2((old - new) * C) + mm(values, p)
                old = new
            return acc, old

        acc, top = lax.fori_loop(0, 8, chunk, (jnp.zeros((128, 256), F32), jnp.full((1, 256), -jnp.inf, F32)))
        acc_ref[:, cols] = acc
        top_ref[:, cols] = jnp.broadcast_to(top, (8, 256))
        return carry

    lax.fori_loop(0, q_ref.shape[1] // 256, tile, 0)


def finish(q_ref, chunks, kv_s, acc_ref, top_ref):
    total = acc_ref[0:1, :]
    fits = jnp.where((total >= T_LOW) & (total <= T_HIGH), 1.0, 0.0)

    @pl.when(jnp.min(fits) < 0.5)
    def _():
        exact(q_ref, chunks, kv_s, acc_ref, top_ref)


def tiles_of(q_ref, acc_in, chunks, acc_ref, top_ref):
    def tile(t, carry):
        cols = pl.ds(pl.multiple_of(t * TQ, TQ), TQ)
        rhs, shift = augmented(q_ref[0:64, cols], q_ref[64:80, cols])
        if acc_in is None:
            acc = jnp.zeros((128, TQ), F32)
        else:
            rows = acc_in[:, cols]
            acc = jnp.concatenate([jnp.broadcast_to(rows[0:1], (56, TQ)), rows], axis=0)
        acc = attend(rhs, chunks, acc)
        if top_ref is None:
            acc_ref[:, cols] = acc[56:128]
        else:
            acc_ref[:, cols] = acc
            top_ref[:, cols] = jnp.broadcast_to(shift, (8, TQ))
        return carry

    lax.fori_loop(0, q_ref.shape[1] // TQ, tile, 0)


def gather_queries(qs, q_s):
    for t in range(3):
        q_s[:, t * GRP:(t + 1) * GRP] = qs[t][...]


def start_kernel(qx, kv, acc):
    tiles_of(qx, None, [kv], acc, None)


def remote_kernel(count, first, last, *refs):
    refs = list(refs)
    qs, refs = refs[:3], refs[3:]
    chunks, refs = refs[:count], refs[count:]
    before, refs = (refs[:8 - count], refs[8 - count:]) if last else ([], refs)
    acc_in = None
    if not first:
        acc_in, refs = refs[0], refs[1:]
    if not last:
        acc, q_s = refs
        gather_queries(qs, q_s)
        tiles_of(q_s, acc_in, chunks, acc, None)
        return
    out0, out1, out2, q_s, acc_s, top_s, kv_s = refs
    gather_queries(qs, q_s)
    tiles_of(q_s, acc_in, chunks, acc_s, top_s)
    finish(q_s, before + chunks, kv_s, acc_s, top_s)
    for t, out in enumerate((out0, out1, out2)):
        cols = slice(t * GRP, (t + 1) * GRP)
        out[0:64, :] = acc_s[64:128, cols].astype(BF)
        out[64:80, :] = stats_rows(acc_s[0:1, cols], top_s[0:1, cols])


def own_kernel(count, *refs):
    qx, own_kv = refs[0], refs[1]
    chunks = list(refs[2:2 + count])
    acc_in, out, acc_s, top_s, kv_s = refs[2 + count:]
    tiles_of(qx, acc_in, chunks, acc_s, top_s)
    finish(qx, [own_kv] + chunks, kv_s, acc_s, top_s)
    out[0:64, :] = acc_s[64:128, :]
    out[64:72, :] = jnp.broadcast_to(acc_s[0:1, :], (8, GRP))
    out[72:80, :] = top_s[...]


def combine_kernel(pos, own, r1, r2, r3, out):
    y, core = pos[0], pos[1]
    sums = [own[0:64, :]] + [r[0:64, :].astype(F32) for r in (r1, r2, r3)]
    stats = [(own[64:65, :], own[72:73, :])] + [stats_read(r[64:80, :]) for r in (r1, r2, r3)]
    top = functools.reduce(jnp.maximum, [s[1] for s in stats])
    factors = [jnp.exp2((s[1] - top) * C) for s in stats]
    total = sum(f * s[0] for f, s in zip(factors, stats))
    context = (sum(f * s for f, s in zip(factors, sums)) / total).astype(BF)
    for i in range(4):
        to_y = lax.rem(y + 4 - i, 4)
        for j in range(2):
            to_core = core if j == 0 else 1 - core
            to = lax.rem(to_y, 2) * 4 + lax.div(to_y, 2) * 2 + to_core
            out[to] = context[:, (2 * i + j) * 128:(2 * i + j + 1) * 128]


def expand_kernel(ctx, frames, w_out, gain, w_expand, hidden, glu, head, tail, wo, we, sems):
    copies = [pltpu.make_async_copy(w_out, wo, sems.at[0])]
    for i in range(4):
        block = i % 2 * 1024 + i // 2 * 512
        copies.append(pltpu.make_async_copy(
            w_expand.at[:, block:block + 512], we.at[:, block:block + 512], sems.at[1 + i]))
    for copy in copies:
        copy.start()
    order = [yy % 2 * 4 + yy // 2 * 2 + cc for cc in range(2) for yy in range(4)]
    context = jnp.concatenate([ctx[s] for s in order], axis=0).T
    copies[0].wait()
    h = (frames[...].astype(F32) + mm(context, wo[...])).astype(BF)
    hidden[...] = h
    normed = norm_rows(h, gain[...]).astype(BF)
    for i in range(2):
        copies[1 + 2 * i].wait()
        value = mm(normed, we[:, i * 512:(i + 1) * 512])
        copies[2 + 2 * i].wait()
        gate = mm(normed, we[:, 1024 + i * 512:1024 + (i + 1) * 512])
        g = (value * jax.nn.sigmoid(gate)).astype(BF)
        cols = slice(i * 512, (i + 1) * 512)
        glu[:, cols] = g
        head[:, cols] = g[:16]
        tail[:, cols] = g[OWN - 16:]


def conv_kernel(before, glu, after, hidden, taps, scale, shift, w_project, out, pad, act, wp, sem):
    copy = pltpu.make_async_copy(w_project, wp, sem)
    copy.start()
    pad[0:16, :] = before[...].astype(F32)
    pad[16:16 + OWN, :] = glu[...].astype(F32)
    pad[16 + OWN:32 + OWN, :] = after[...].astype(F32)

    def block(i, carry):
        cols = pl.ds(pl.multiple_of(i * 128, 128), 128)
        conv = jnp.zeros((OWN, 128), F32)
        for tap in range(31):
            conv = conv + taps[tap:tap + 1, cols] * pad[1 + tap:1 + tap + OWN, cols]
        act[:, cols] = jax.nn.silu(scale[:, cols] * conv + shift[:, cols]).astype(BF)
        return carry

    lax.fori_loop(0, D // 128, block, 0)
    copy.wait()
    out[...] = (hidden[...].astype(F32) + mm(act[...], wp[...])).astype(BF)


def body(frames, gain_attn, w_query, w_key, w_value, w_out, gain_conv, w_expand, kernel_taps, bn_scale, bn_shift, w_project):
    core = lax.axis_index("core")
    y = lax.axis_index("yhi") * 2 + lax.axis_index("ylo")
    pos = jnp.stack([y, core]).astype(jnp.int32)

    def along(axis, value, step):
        count = lax.axis_size(axis)
        return lax.ppermute(value, axis, [(i, (i + step) % count) for i in range(count)])

    def along_y(value, step):
        place_of = lambda v: v % 2 * 2 + v // 2
        return lax.ppermute(value, ("ylo", "yhi"), [(place_of(i), place_of((i + step) % 4)) for i in range(4)])

    row = lambda v: v.reshape(1, -1)
    sib = along("core", frames, 1)
    sent = call(
        project_kernel, (pos, frames, sib, row(gain_attn), w_query, w_key, w_value), [SM, VM, VM, VM, ANY, ANY, ANY],
        [((384, 128), BF)] * 4, [pltpu.VMEM((3, D, 256), BF), pltpu.SemaphoreType.DMA((3,))],
    )
    got = [sent[0]] + [along_y(sent[i], i) for i in (1, 2, 3)]
    kv, qx = call(pack_kernel, got, [VM] * 4, [((GRP, 128), BF), ((80, GRP), BF)])
    up1, down1 = along("z", kv, 1), along("z", kv, -1)
    queries = [along("x", qx, i) for i in (1, 2, 3)]
    own_acc, = call(start_kernel, (qx, kv), [VM] * 2, [((72, GRP), F32)], us=2)
    up1, down1, own_acc = lax.optimization_barrier((up1, down1, own_acc))
    up2, down2 = along("z", up1, 1), along("z", down1, -1)
    many = ((72, 3 * GRP), F32)
    q_scratch = pltpu.VMEM((80, 3 * GRP), BF)
    acc, = call(
        functools.partial(remote_kernel, 3, True, False), (*queries, kv, up1, down1), [VM] * 6, [many], [q_scratch], us=10,
    )
    up2, down2, acc = lax.optimization_barrier((up2, down2, acc))
    up3, down3 = along("z", up2, 1), along("z", down2, -1)
    acc, = call(
        functools.partial(remote_kernel, 2, False, False), (*queries, up2, down2, acc), [VM] * 6, [many], [q_scratch], us=7,
    )
    up3, down3, acc = lax.optimization_barrier((up3, down3, acc))
    up4 = along("z", up3, 1)
    acc, = call(
        functools.partial(remote_kernel, 2, False, False), (*queries, up3, down3, acc), [VM] * 6, [many], [q_scratch], us=7,
    )
    parts = call(
        functools.partial(remote_kernel, 1, False, True),
        (*queries, up4, kv, up1, down1, up2, down2, up3, down3, acc), [VM] * 4 + [ANY] * 7 + [VM],
        [((80, GRP), BF)] * 3,
        [q_scratch, pltpu.VMEM((128, 3 * GRP), F32), pltpu.VMEM((8, 3 * GRP), F32), pltpu.VMEM((8, GRP, 128), BF)],
        us=4,
    )
    returned = [along("x", parts[i - 1], -i) for i in (1, 2, 3)]
    chunks = (up1, down1, up2, down2, up3, down3, up4)
    own_part, = call(
        functools.partial(own_kernel, 7), (qx, kv, *chunks, own_acc), [VM] * 10, [((80, GRP), F32)],
        [pltpu.VMEM((128, GRP), F32), pltpu.VMEM((8, GRP), F32), pltpu.VMEM((8, GRP, 128), BF)], us=8,
    )
    contexts, = call(combine_kernel, (pos, own_part, *returned), [SM] + [VM] * 4, [((8, HD, 128), BF)])
    contexts = lax.all_to_all(contexts, YC, 0, 0)
    hidden, glu, head, tail = call(
        expand_kernel, (contexts, frames, w_out, row(gain_conv), w_expand), [VM, VM, ANY, VM, ANY],
        [((OWN, D), BF), ((OWN, D), BF), ((16, D), BF), ((16, D), BF)],
        [pltpu.VMEM((512, D), BF), pltpu.VMEM((D, 2 * D), BF), pltpu.SemaphoreType.DMA((5,))],
    )
    count = lax.axis_size(NAMES)
    before = lax.ppermute(tail, NAMES, [(i, i + 1) for i in range(count - 1)])
    after = lax.ppermute(head, NAMES, [(i + 1, i) for i in range(count - 1)])
    out, = call(
        conv_kernel, (before, glu, after, hidden, kernel_taps, row(bn_scale), row(bn_shift), w_project),
        [VM] * 7 + [ANY], [((OWN, D), BF)],
        [pltpu.VMEM((OWN + 32, D), F32), pltpu.VMEM((OWN, D), BF), pltpu.VMEM((D, D), BF), pltpu.SemaphoreType.DMA],
    )
    return out


def solution(mesh):
    fine = Mesh(mesh.devices.reshape(2, 8, 4, 2, 2), NAMES)
    rows = P(NAMES, None)
    return jax.shard_map(
        body, mesh=fine, in_specs=(rows,) + (P(),) * 11, out_specs=rows, check_vma=False,
    )
```

time: 1130 us -> 249 us (0.22)
  waiting for transfers between devices: 595 us -> 14 us
  matrix products: 275 us -> 0 us
  Pallas kernels: 0 us -> 187 us
  other arithmetic: 141 us -> 0.59 us
  local copies, waits for them, and re-layouts: 53.5 us -> 5.34 us
  starting transfers between devices: 50.3 us -> 27.7 us
  blocking collectives: 0 us -> 13.6 us
  between operations: 13.3 us -> 0.35 us
    all_gather x3 -> x0, waiting for transfers between devices: 585 us -> none  [the longest x1 290 us: body(): lax.all_gather(value_local, 'outer', axis=0, tiled=True)]
    dot_general x132 -> x0, matrix products: 275 us -> none  [the longest x64 175 us: one_block(): jnp.einsum('qhd,khd->qhk', query_heads, key_block, preferred_element_type...]
    pallas_call x0 -> x11, Pallas kernels: none -> 187 us  [call(): pl.pallas_call(kernel, in_specs=specs, out_specs=[VM] * len(outs), out_sh...]
    reduce_sum x67 -> x0, other arithmetic: 137 us -> none  [the longest x64 134 us: one_block(): total = total * factor + jnp.sum(weights, axis=-1)]
    all_to_all x1 -> x0, starting transfers between devices: 45.4 us -> none  [body(): lax.all_to_all(context_local, 'inner', split_axis=0, concat_axis=1, tiled...]
    unnamed x20 -> x38, local copies, waits for them, and re-layouts: 44.1 us -> 5.34 us
    ppermute x2 -> x19, starting transfers between devices: 4.84 us -> 27.7 us  [the longest x14 18.9 us: along(): lax.ppermute(value, axis, [(i, (i + step) % count) for i in range(count)])]
    all_to_all x0 -> x1, blocking collectives: none -> 13.6 us  [body(): contexts = lax.all_to_all(contexts, YC, 0, 0)]
  transfers between devices with their start and end apart: 6 -> 19, of which waited for: 5 -> 7; matrix products, arithmetic and copies ran while one was open for 2% -> 0% of each run, Pallas kernels for 0% -> 28%
where the time goes in v1:
time: 249 us; the launch traced here: 248 us
  Pallas kernels  187 us (75%)
  starting transfers between devices  27.7 us (11%)
  waiting for transfers between devices  14 us (6%)
  blocking collectives  13.6 us (5%)
  local copies, waits for them, and re-layouts  5.34 us (2%)
    pallas_call x11, Pallas kernels, call(): pl.pallas_call(kernel, in_specs=specs, out_specs=[VM] * len(outs), out_sh...  187 us
    ppermute x14, starting transfers between devices, along(): lax.ppermute(value, axis, [(i, (i + step) % count) for i in range(count)])  18.9 us
    all_to_all x1, blocking collectives, body(): contexts = lax.all_to_all(contexts, YC, 0, 0)  13.6 us
    unnamed x38, local copies, waits for them, and re-layouts  5.34 us
    ppermute x1, waiting for transfers between devices, body(): after = lax.ppermute(head, NAMES, [(i + 1, i) for i in range(count - 1)])  5 us
  transfers between devices with their start and end apart: 19, of which 7 were waited for; matrix products, arithmetic and copies ran while one was open for 0% of the time, Pallas kernels for 28%

profile of v1, /device:TPU:1, one launch (start us, length us, event | category | flops | bytes accessed | tf_op | source)
XLA Modules:
  0.0 248.2 jit_solution(8062246059345121852)
XLA Ops:
  0.0 3.2 %collective-permute-start = (bf16[128,1024]{1,0:T(8,128)(2,1)}, bf16[128,1024]{1,0:T(8,128)(2,1)S(1)}, u32[]{:S(2)}, u32[]{:S(2)}) collective-permute-start(bf16[128,1024]{1,0:T(8,128)(2,1)} %frames.1), channel_id=1, source_target_pairs={{0,1},{1,0},{2,3},{3,2},{4,5},{5,4},{6,7},{7,6},{8,9},{9,8},{10,11... | collective-permute-start | bytes 786440 | tf_op jit(solution)/shard_map/ppermute | solution.py:330
  3.2 0.6 pad_add_fusion.pos
  3.8 0.8 collective-permute-done.sib
  4.6 0.7 copy-done.7
  5.3 4.2 %shard_map.118 = (bf16[384,128]{1,0:T(8,128)(2,1)}, bf16[384,128]{1,0:T(8,128)(2,1)}, bf16[384,128]{1,0:T(8,128)(2,1)}, bf16[384,128]{1,0:T(8,128)(2,1)}) custom-call(s32[2]{0:T(128)} %pad_add_fusion.pos, bf16[128,1024]{1,0:T(8,128)(2,1)} %frames.1, bf16[128,1024]{1,0:T(8,128)(2,1)} %copy-done.7, f32[1,1024]{1,0:T(1,128)} %bitcast.6, bf16[1024,512]{1,0:T(8,128)(2,1)} %wq.1, ...), custom_call_target="tpu_custom_call" | custom-call | flops 2000000000 | bytes 1024 | tf_op jit(solution)/shard_map/pallas_call | solution.py:30
  9.5 0.1 collective-permute-start.1
  9.6 2.2 collective-permute-start.2
  11.8 1.1 collective-permute-start.3
  12.8 2.7 %collective-permute-done.1.a1 = bf16[384,128]{1,0:T(8,128)(2,1)S(1)} collective-permute-done((bf16[384,128]{1,0:T(8,128)(2,1)}, bf16[384,128]{1,0:T(8,128)(2,1)S(1)}, u32[]{:S(2)}, u32[]{:S(2)}) %collective-permute-start.1) | collective-permute-done | bytes 98336 | tf_op jit(solution)/shard_map/ppermute | solution.py:334
  15.5 1.1 collective-permute-done.2.a2
  16.6 0.7 collective-permute-done.3.a3
  17.4 0.6 copy-done.16
  18.0 2.2 shard_map.119
  20.2 4.9 %collective-permute-start.5 = (bf16[1024,128]{1,0:T(8,128)(2,1)}, bf16[1024,128]{1,0:T(8,128)(2,1)S(1)}, u32[]{:S(2)}, u32[]{:S(2)}) collective-permute-start(bf16[1024,128]{1,0:T(8,128)(2,1)} %get-tuple-element.32.kv.refs_3_.refs_1_.refs_4_), channel_id=1, source_target_pairs={{0,112},{16,0},{32,16},{48,32},{64,48},{80,64},{96,80},{112,96},{1... | collective-permute-start | bytes 786440 | tf_op jit(solution)/shard_map/ppermute | solution.py:330
  25.0 2.5 %collective-permute-start.10 = (bf16[80,1024]{1,0:T(8,128)(2,1)}, bf16[80,1024]{1,0:T(8,128)(2,1)S(1)}, u32[]{:S(2)}, u32[]{:S(2)}) collective-permute-start(bf16[80,1024]{1,0:T(8,128)(2,1)} %get-tuple-element.31.qx.refs_0_), channel_id=1, source_target_pairs={{0,12},{4,0},{8,4},{12,8},{1,13},{5,1},{9,5},{13,9},{2,14},{6,2},{... | collective-permute-start | bytes 491528 | tf_op jit(solution)/shard_map/ppermute | solution.py:330
  27.5 0.5 collective-permute-start.9
  28.0 0.6 collective-permute-start.8
  28.6 3.1 %shard_map.120.refs_9_ = f32[72,1024]{1,0:T(8,128)} custom-call(bf16[80,1024]{1,0:T(8,128)(2,1)} %get-tuple-element.31.qx.refs_0_, bf16[1024,128]{1,0:T(8,128)(2,1)} %get-tuple-element.32.kv.refs_3_.refs_1_.refs_4_), custom_call_target="tpu_custom_call" | custom-call | flops 2000000000 | bytes 1024 | tf_op jit(solution)/shard_map/pallas_call | solution.py:30
  31.8 0.0 collective-permute-done.5.refs_5_.refs_3_.refs_6_
  31.8 1.0 collective-permute-done.4.refs_4_.refs_2_.refs_5_
  32.8 2.7 %collective-permute-start.7 = (bf16[1024,128]{1,0:T(8,128)(2,1)S(1)}, bf16[1024,128]{1,0:T(8,128)(2,1)S(1)}, u32[]{:S(2)}, u32[]{:S(2)}) collective-permute-start(bf16[1024,128]{1,0:T(8,128)(2,1)S(1)} %collective-permute-done.5.refs_5_.refs_3_.refs_6_), channel_id=1, source_target_pairs={{0,112},{16,0},{32,16},{48,32},{64,48},{80,64},{96,80},{112,96},{1... | collective-permute-start | bytes 786440 | tf_op jit(solution)/shard_map/ppermute | solution.py:330
  35.5 2.7 %collective-permute-done.8.refs_0_ = bf16[80,1024]{1,0:T(8,128)(2,1)S(1)} collective-permute-done((bf16[80,1024]{1,0:T(8,128)(2,1)}, bf16[80,1024]{1,0:T(8,128)(2,1)S(1)}, u32[]{:S(2)}, u32[]{:S(2)}) %collective-permute-start.8) | collective-permute-done | bytes 163872 | tf_op jit(solution)/shard_map/ppermute | solution.py:330
  38.2 0.7 copy-done.10
  38.8 10.8 %shard_map.121.refs_5_ = f32[72,3072]{1,0:T(8,128)} custom-call(bf16[80,1024]{1,0:T(8,128)(2,1)} %copy-done.10, bf16[80,1024]{1,0:T(8,128)(2,1)} %copy-done.9, bf16[80,1024]{1,0:T(8,128)(2,1)} %copy-done.8, bf16[1024,128]{1,0:T(8,128)(2,1)} %get-tuple-element.32.kv.refs_3_.refs_1_.refs_4_, bf16[1024,128]{1,0:T(8,128)(2,1)} %copy-done.1, ...), custom_call_target="tpu_custom_call" | custom-call | flops 10000000000 | bytes 1024 | tf_op jit(solution)/shard_map/pallas_call | solution.py:30
  49.7 0.1 collective-permute-start.11
  49.8 2.7 %collective-permute-start.12 = (bf16[1024,128]{1,0:T(8,128)(2,1)S(1)}, bf16[1024,128]{1,0:T(8,128)(2,1)S(1)}, u32[]{:S(2)}, u32[]{:S(2)}) collective-permute-start(bf16[1024,128]{1,0:T(8,128)(2,1)S(1)} %collective-permute-done.7.refs_4_.refs_5_.refs_8_), channel_id=1, source_target_pairs={{0,112},{16,0},{32,16},{48,32},{64,48},{80,64},{96,80},{112,96},{1... | collective-permute-start | bytes 786440 | tf_op jit(solution)/shard_map/ppermute | solution.py:330
  52.4 8.5 %shard_map.122.refs_5_ = f32[72,3072]{1,0:T(8,128)} custom-call(bf16[80,1024]{1,0:T(8,128)(2,1)} %copy-done.10, bf16[80,1024]{1,0:T(8,128)(2,1)} %copy-done.9, bf16[80,1024]{1,0:T(8,128)(2,1)} %copy-done.8, bf16[1024,128]{1,0:T(8,128)(2,1)} %copy-done.2, bf16[1024,128]{1,0:T(8,128)(2,1)} %copy-done.3, f32[72,3072]{1,0:T(8,128)} %shard_map.121.refs_5_), custom_call_target="tpu_custom_call" | custom-call | flops 7000000000 | bytes 1024 | tf_op jit(solution)/shard_map/pallas_call | solution.py:30
  61.0 0.1 collective-permute-start.13
  61.1 0.6 copy-done.4
  61.7 0.1 copy-done.5
  61.7 8.5 %shard_map.124.refs_11_ = f32[72,3072]{1,0:T(8,128)} custom-call(bf16[80,1024]{1,0:T(8,128)(2,1)} %copy-done.10, bf16[80,1024]{1,0:T(8,128)(2,1)} %copy-done.9, bf16[80,1024]{1,0:T(8,128)(2,1)} %copy-done.8, bf16[1024,128]{1,0:T(8,128)(2,1)} %copy-done.4, bf16[1024,128]{1,0:T(8,128)(2,1)} %copy-done.5, f32[72,3072]{1,0:T(8,128)} %shard_map.122.refs_5_), custom_call_target="tpu_custom_call" | custom-call | flops 7000000000 | bytes 1024 | tf_op jit(solution)/shard_map/pallas_call | solution.py:30
  70.3 0.7 copy-done.6
  71.0 99.5 %shard_map.125 = (bf16[80,1024]{1,0:T(8,128)(2,1)}, bf16[80,1024]{1,0:T(8,128)(2,1)}, bf16[80,1024]{1,0:T(8,128)(2,1)}) custom-call(bf16[80,1024]{1,0:T(8,128)(2,1)} %copy-done.10, bf16[80,1024]{1,0:T(8,128)(2,1)} %copy-done.9, bf16[80,1024]{1,0:T(8,128)(2,1)} %copy-done.8, bf16[1024,128]{1,0:T(8,128)(2,1)} %copy-done.6, ...), custom_call_target="tpu_custom_call" | custom-call | flops 4000000000 | bytes 1024 | tf_op jit(solution)/shard_map/pallas_call | solution.py:30
  170.5 0.5 collective-permute-start.14
  171.0 0.5 collective-permute-start.15
  171.5 0.6 collective-permute-start.16
  172.1 37.7 %shard_map.123.own = f32[80,1024]{1,0:T(8,128)} custom-call(bf16[80,1024]{1,0:T(8,128)(2,1)} %get-tuple-element.31.qx.refs_0_, bf16[1024,128]{1,0:T(8,128)(2,1)} %get-tuple-element.32.kv.refs_3_.refs_1_.refs_4_, bf16[1024,128]{1,0:T(8,128)(2,1)} %copy-done.1, bf16[1024,128]{1,0:T(8,128)(2,1)} %copy-done, bf16[1024,128]{1,0:T(8,128)(2,1)} %copy-done.2, ...), custom_call_target="tpu_custom_call" | custom-call | flops 8000000000 | bytes 1024 | tf_op jit(solution)/shard_map/pallas_call | solution.py:30
  209.9 0.6 copy-done.11
  210.5 0.0 copy-done.12
  210.5 0.7 copy-done.13
  211.2 2.0 shard_map.126
  213.2 13.6 %all_to_all.5.ctx = bf16[8,64,128]{2,1,0:T(8,128)(2,1)} all-to-all(bf16[8,64,128]{2,1,0:T(8,128)(2,1)} %shard_map.126), channel_id=1, replica_groups=mesh['ylo'=2,'z'=8,'x'=4,'yhi'=2,'core'=2] {'ylo','yhi','core'}, dimensions={0} | all-to-all | bytes 262144 | tf_op jit(solution)/shard_map/all_to_all | solution.py:378
  226.8 4.8 %shard_map.127 = (bf16[128,1024]{1,0:T(8,128)(2,1)}, bf16[128,1024]{1,0:T(8,128)(2,1)}, bf16[16,1024]{1,0:T(8,128)(2,1)}, bf16[16,1024]{1,0:T(8,128)(2,1)}) custom-call(bf16[8,64,128]{2,1,0:T(8,128)(2,1)} %all_to_all.5.ctx, bf16[128,1024]{1,0:T(8,128)(2,1)} %frames.1, bf16[512,1024]{1,0:T(8,128)(2,1)} %w_out.1, f32[1,1024]{1,0:T(1,128)} %bitcast.7, ...), custom_call_target="tpu_custom_call" | custom-call | flops 2000000000 | bytes 1024 | tf_op jit(solution)/shard_map/pallas_call | solution.py:30
  231.6 3.6 %collective-permute-start.17 = (bf16[16,1024]{1,0:T(8,128)(2,1)}, bf16[16,1024]{1,0:T(8,128)(2,1)S(1)}, u32[]{:S(2)}, u32[]{:S(2)}) collective-permute-start(bf16[16,1024]{1,0:T(8,128)(2,1)} %get-tuple-element.45), channel_id=1, source_target_pairs={{0,1},{1,2},{2,3},{3,4},{4,5},{5,6},{6,7},{7,8},{8,9},{9,10},{10,1... | collective-permute-start | bytes 98312 | tf_op jit(solution)/shard_map/ppermute | solution.py:385
  235.2 1.9 collective-permute-start.18
  237.1 5.0 %collective-permute-done.18.after = bf16[16,1024]{1,0:T(8,128)(2,1)S(1)} collective-permute-done((bf16[16,1024]{1,0:T(8,128)(2,1)}, bf16[16,1024]{1,0:T(8,128)(2,1)S(1)}, u32[]{:S(2)}, u32[]{:S(2)}) %collective-permute-start.18) | collective-permute-done | bytes 32800 | tf_op jit(solution)/shard_map/ppermute | solution.py:386
  242.1 0.6 copy-done.18
  242.7 5.3 %shard_map.128 = bf16[128,1024]{1,0:T(8,128)(2,1)} custom-call(bf16[16,1024]{1,0:T(8,128)(2,1)} %copy-done.17, bf16[128,1024]{1,0:T(8,128)(2,1)} %get-tuple-element.46.glu, bf16[16,1024]{1,0:T(8,128)(2,1)} %copy-done.18, bf16[128,1024]{1,0:T(8,128)(2,1)} %get-tuple-element.48.hidden, f32[31,1024]{1,0:T(8,128)} %taps.1, f32[1,1024]{1,0:T(1,128)} %bitcast.8, ...), custom_call_target="tpu_custom_call" | custom-call | flops 2000000000 | bytes 1024 | tf_op jit(solution)/shard_map/pallas_call | solution.py:30
  (41 shorter events, 0.1 us)
Async XLA Ops:
  0.0 4.6 %collective-permute-start = (bf16[128,1024]{1,0:T(8,128)(2,1)}, bf16[128,1024]{1,0:T(8,128)(2,1)S(1)}, u32[]{:S(2)}, u32[]{:S(2)}) collective-permute-start(bf16[128,1024]{1,0:T(8,128)(2,1)} %frames.1), channel_id=1, source_target_pairs={{0,1},{1,0},{2,3},{3,2},{4,5},{5,4},{6,7},{7,6},{8,9},{9,8},{10,11... | collective-permute-start | bytes 786440 | tf_op jit(solution)/shard_map/ppermute | solution.py:330
  4.6 0.7 copy-start.7
  9.5 6.0 %collective-permute-start.1 = (bf16[384,128]{1,0:T(8,128)(2,1)}, bf16[384,128]{1,0:T(8,128)(2,1)S(1)}, u32[]{:S(2)}, u32[]{:S(2)}) collective-permute-start(bf16[384,128]{1,0:T(8,128)(2,1)} %get-tuple-element.28), channel_id=1, source_target_pairs={{0,128},{128,2},{2,130},{130,0},{1,129},{129,3},{3,131},{131,1},{4... | collective-permute-start | bytes 294920 | tf_op jit(solution)/shard_map/ppermute | solution.py:334
  9.6 7.0 %collective-permute-start.2 = (bf16[384,128]{1,0:T(8,128)(2,1)}, bf16[384,128]{1,0:T(8,128)(2,1)S(1)}, u32[]{:S(2)}, u32[]{:S(2)}) collective-permute-start(bf16[384,128]{1,0:T(8,128)(2,1)} %get-tuple-element.29), channel_id=1, source_target_pairs={{0,2},{128,130},{2,0},{130,128},{1,3},{129,131},{3,1},{131,129},{4... | collective-permute-start | bytes 294920 | tf_op jit(solution)/shard_map/ppermute | solution.py:334
  11.8 5.6 %collective-permute-start.3 = (bf16[384,128]{1,0:T(8,128)(2,1)}, bf16[384,128]{1,0:T(8,128)(2,1)S(1)}, u32[]{:S(2)}, u32[]{:S(2)}) collective-permute-start(bf16[384,128]{1,0:T(8,128)(2,1)} %get-tuple-element.30), channel_id=1, source_target_pairs={{0,130},{128,0},{2,128},{130,2},{1,131},{129,1},{3,129},{131,3},{4... | collective-permute-start | bytes 294920 | tf_op jit(solution)/shard_map/ppermute | solution.py:334
  15.5 1.8 copy-start.14
  16.6 0.8 copy-start.15
  17.4 0.6 copy-start.16
  20.2 11.6 %collective-permute-start.5 = (bf16[1024,128]{1,0:T(8,128)(2,1)}, bf16[1024,128]{1,0:T(8,128)(2,1)S(1)}, u32[]{:S(2)}, u32[]{:S(2)}) collective-permute-start(bf16[1024,128]{1,0:T(8,128)(2,1)} %get-tuple-element.32.kv.refs_3_.refs_1_.refs_4_), channel_id=1, source_target_pairs={{0,112},{16,0},{32,16},{48,32},{64,48},{80,64},{96,80},{112,96},{1... | collective-permute-start | bytes 786440 | tf_op jit(solution)/shard_map/ppermute | solution.py:330
  25.0 7.7 %collective-permute-start.4 = (bf16[1024,128]{1,0:T(8,128)(2,1)}, bf16[1024,128]{1,0:T(8,128)(2,1)S(1)}, u32[]{:S(2)}, u32[]{:S(2)}) collective-permute-start(bf16[1024,128]{1,0:T(8,128)(2,1)} %get-tuple-element.32.kv.refs_3_.refs_1_.refs_4_), channel_id=1, source_target_pairs={{0,16},{16,32},{32,48},{48,64},{64,80},{80,96},{96,112},{112,0},{1... | collective-permute-start | bytes 786440 | tf_op jit(solution)/shard_map/ppermute | solution.py:330
  25.0 10.4 %collective-permute-start.10 = (bf16[80,1024]{1,0:T(8,128)(2,1)}, bf16[80,1024]{1,0:T(8,128)(2,1)S(1)}, u32[]{:S(2)}, u32[]{:S(2)}) collective-permute-start(bf16[80,1024]{1,0:T(8,128)(2,1)} %get-tuple-element.31.qx.refs_0_), channel_id=1, source_target_pairs={{0,12},{4,0},{8,4},{12,8},{1,13},{5,1},{9,5},{13,9},{2,14},{6,2},{... | collective-permute-start | bytes 491528 | tf_op jit(solution)/shard_map/ppermute | solution.py:330
  27.5 7.9 %collective-permute-start.9 = (bf16[80,1024]{1,0:T(8,128)(2,1)}, bf16[80,1024]{1,0:T(8,128)(2,1)S(1)}, u32[]{:S(2)}, u32[]{:S(2)}) collective-permute-start(bf16[80,1024]{1,0:T(8,128)(2,1)} %get-tuple-element.31.qx.refs_0_), channel_id=1, source_target_pairs={{0,8},{4,12},{8,0},{12,4},{1,9},{5,13},{9,1},{13,5},{2,10},{6,14},... | collective-permute-start | bytes 491528 | tf_op jit(solution)/shard_map/ppermute | solution.py:330
  28.0 10.1 %collective-permute-start.8 = (bf16[80,1024]{1,0:T(8,128)(2,1)}, bf16[80,1024]{1,0:T(8,128)(2,1)S(1)}, u32[]{:S(2)}, u32[]{:S(2)}) collective-permute-start(bf16[80,1024]{1,0:T(8,128)(2,1)} %get-tuple-element.31.qx.refs_0_), channel_id=1, source_target_pairs={{0,4},{4,8},{8,12},{12,0},{1,5},{5,9},{9,13},{13,1},{2,6},{6,10},{... | collective-permute-start | bytes 491528 | tf_op jit(solution)/shard_map/ppermute | solution.py:330
  31.8 6.4 %copy-start = (bf16[1024,128]{1,0:T(8,128)(2,1)}, bf16[1024,128]{1,0:T(8,128)(2,1)S(1)}, u32[]{:S(2)}) copy-start(bf16[1024,128]{1,0:T(8,128)(2,1)S(1)} %collective-permute-done.5.refs_5_.refs_3_.refs_6_) | copy-start | bytes 786436
  32.8 5.4 %copy-start.1 = (bf16[1024,128]{1,0:T(8,128)(2,1)}, bf16[1024,128]{1,0:T(8,128)(2,1)S(1)}, u32[]{:S(2)}) copy-start(bf16[1024,128]{1,0:T(8,128)(2,1)S(1)} %collective-permute-done.4.refs_4_.refs_2_.refs_5_) | copy-start | bytes 786436
  32.8 16.9 %collective-permute-start.6 = (bf16[1024,128]{1,0:T(8,128)(2,1)S(1)}, bf16[1024,128]{1,0:T(8,128)(2,1)S(1)}, u32[]{:S(2)}, u32[]{:S(2)}) collective-permute-start(bf16[1024,128]{1,0:T(8,128)(2,1)S(1)} %collective-permute-done.4.refs_4_.refs_2_.refs_5_), channel_id=1, source_target_pairs={{0,16},{16,32},{32,48},{48,64},{64,80},{80,96},{96,112},{112,0},{1... | collective-permute-start | bytes 786440 | tf_op jit(solution)/shard_map/ppermute | solution.py:330
  32.8 16.9 %collective-permute-start.7 = (bf16[1024,128]{1,0:T(8,128)(2,1)S(1)}, bf16[1024,128]{1,0:T(8,128)(2,1)S(1)}, u32[]{:S(2)}, u32[]{:S(2)}) collective-permute-start(bf16[1024,128]{1,0:T(8,128)(2,1)S(1)} %collective-permute-done.5.refs_5_.refs_3_.refs_6_), channel_id=1, source_target_pairs={{0,112},{16,0},{32,16},{48,32},{64,48},{80,64},{96,80},{112,96},{1... | collective-permute-start | bytes 786440 | tf_op jit(solution)/shard_map/ppermute | solution.py:330
  35.4 2.7 %copy-start.8 = (bf16[80,1024]{1,0:T(8,128)(2,1)}, bf16[80,1024]{1,0:T(8,128)(2,1)S(1)}, u32[]{:S(2)}) copy-start(bf16[80,1024]{1,0:T(8,128)(2,1)S(1)} %collective-permute-done.10.refs_2_) | copy-start | bytes 491524
  35.5 2.7 %copy-start.9 = (bf16[80,1024]{1,0:T(8,128)(2,1)}, bf16[80,1024]{1,0:T(8,128)(2,1)S(1)}, u32[]{:S(2)}) copy-start(bf16[80,1024]{1,0:T(8,128)(2,1)S(1)} %collective-permute-done.9.refs_1_) | copy-start | bytes 491524
  38.2 0.7 copy-start.10
  49.7 2.8 %copy-start.2 = (bf16[1024,128]{1,0:T(8,128)(2,1)}, bf16[1024,128]{1,0:T(8,128)(2,1)S(1)}, u32[]{:S(2)}) copy-start(bf16[1024,128]{1,0:T(8,128)(2,1)S(1)} %collective-permute-done.6.refs_3_.refs_4_.refs_7_) | copy-start | bytes 786436
  49.7 2.8 %copy-start.3 = (bf16[1024,128]{1,0:T(8,128)(2,1)}, bf16[1024,128]{1,0:T(8,128)(2,1)S(1)}, u32[]{:S(2)}) copy-start(bf16[1024,128]{1,0:T(8,128)(2,1)S(1)} %collective-permute-done.7.refs_4_.refs_5_.refs_8_) | copy-start | bytes 786436
  49.7 11.3 %collective-permute-start.11 = (bf16[1024,128]{1,0:T(8,128)(2,1)S(1)}, bf16[1024,128]{1,0:T(8,128)(2,1)S(1)}, u32[]{:S(2)}, u32[]{:S(2)}) collective-permute-start(bf16[1024,128]{1,0:T(8,128)(2,1)S(1)} %collective-permute-done.6.refs_3_.refs_4_.refs_7_), channel_id=1, source_target_pairs={{0,16},{16,32},{32,48},{48,64},{64,80},{80,96},{96,112},{112,0},{1... | collective-permute-start | bytes 786440 | tf_op jit(solution)/shard_map/ppermute | solution.py:330
  49.8 11.2 %collective-permute-start.12 = (bf16[1024,128]{1,0:T(8,128)(2,1)S(1)}, bf16[1024,128]{1,0:T(8,128)(2,1)S(1)}, u32[]{:S(2)}, u32[]{:S(2)}) collective-permute-start(bf16[1024,128]{1,0:T(8,128)(2,1)S(1)} %collective-permute-done.7.refs_4_.refs_5_.refs_8_), channel_id=1, source_target_pairs={{0,112},{16,0},{32,16},{48,32},{64,48},{80,64},{96,80},{112,96},{1... | collective-permute-start | bytes 786440 | tf_op jit(solution)/shard_map/ppermute | solution.py:330
  61.0 0.7 copy-start.4
  61.0 0.8 copy-start.5
  61.0 9.3 %collective-permute-start.13 = (bf16[1024,128]{1,0:T(8,128)(2,1)S(1)}, bf16[1024,128]{1,0:T(8,128)(2,1)S(1)}, u32[]{:S(2)}, u32[]{:S(2)}) collective-permute-start(bf16[1024,128]{1,0:T(8,128)(2,1)S(1)} %collective-permute-done.11.refs_6_.refs_3_.refs_9_), channel_id=1, source_target_pairs={{0,16},{16,32},{32,48},{48,64},{64,80},{80,96},{96,112},{112,0},{1... | collective-permute-start | bytes 786440 | tf_op jit(solution)/shard_map/ppermute | solution.py:330
  70.3 0.7 copy-start.6
  170.5 39.4 %collective-permute-start.14 = (bf16[80,1024]{1,0:T(8,128)(2,1)}, bf16[80,1024]{1,0:T(8,128)(2,1)S(1)}, u32[]{:S(2)}, u32[]{:S(2)}) collective-permute-start(bf16[80,1024]{1,0:T(8,128)(2,1)} %get-tuple-element.42), channel_id=1, source_target_pairs={{0,12},{4,0},{8,4},{12,8},{1,13},{5,1},{9,5},{13,9},{2,14},{6,2},{... | collective-permute-start | bytes 491528 | tf_op jit(solution)/shard_map/ppermute | solution.py:330
  171.0 38.9 %collective-permute-start.15 = (bf16[80,1024]{1,0:T(8,128)(2,1)}, bf16[80,1024]{1,0:T(8,128)(2,1)S(1)}, u32[]{:S(2)}, u32[]{:S(2)}) collective-permute-start(bf16[80,1024]{1,0:T(8,128)(2,1)} %get-tuple-element.43), channel_id=1, source_target_pairs={{0,8},{4,12},{8,0},{12,4},{1,9},{5,13},{9,1},{13,5},{2,10},{6,14},... | collective-permute-start | bytes 491528 | tf_op jit(solution)/shard_map/ppermute | solution.py:330
  171.5 38.4 %collective-permute-start.16 = (bf16[80,1024]{1,0:T(8,128)(2,1)}, bf16[80,1024]{1,0:T(8,128)(2,1)S(1)}, u32[]{:S(2)}, u32[]{:S(2)}) collective-permute-start(bf16[80,1024]{1,0:T(8,128)(2,1)} %get-tuple-element.44), channel_id=1, source_target_pairs={{0,4},{4,8},{8,12},{12,0},{1,5},{5,9},{9,13},{13,1},{2,6},{6,10},{... | collective-permute-start | bytes 491528 | tf_op jit(solution)/shard_map/ppermute | solution.py:330
  209.8 0.7 copy-start.11
  209.8 0.7 copy-start.12
  210.5 0.7 copy-start.13
  231.6 5.5 %collective-permute-start.17 = (bf16[16,1024]{1,0:T(8,128)(2,1)}, bf16[16,1024]{1,0:T(8,128)(2,1)S(1)}, u32[]{:S(2)}, u32[]{:S(2)}) collective-permute-start(bf16[16,1024]{1,0:T(8,128)(2,1)} %get-tuple-element.45), channel_id=1, source_target_pairs={{0,1},{1,2},{2,3},{3,4},{4,5},{5,6},{6,7},{7,8},{8,9},{9,10},{10,1... | collective-permute-start | bytes 98312 | tf_op jit(solution)/shard_map/ppermute | solution.py:385
  235.2 6.9 %collective-permute-start.18 = (bf16[16,1024]{1,0:T(8,128)(2,1)}, bf16[16,1024]{1,0:T(8,128)(2,1)S(1)}, u32[]{:S(2)}, u32[]{:S(2)}) collective-permute-start(bf16[16,1024]{1,0:T(8,128)(2,1)} %get-tuple-element.47), channel_id=1, source_target_pairs={{1,0},{2,1},{3,2},{4,3},{5,4},{6,5},{7,6},{8,7},{9,8},{10,9},{11,1... | collective-permute-start | bytes 98312 | tf_op jit(solution)/shard_map/ppermute | solution.py:386
  237.1 5.0 %copy-start.17 = (bf16[16,1024]{1,0:T(8,128)(2,1)}, bf16[16,1024]{1,0:T(8,128)(2,1)S(1)}, u32[]{:S(2)}) copy-start(bf16[16,1024]{1,0:T(8,128)(2,1)S(1)} %collective-permute-done.17.before) | copy-start | bytes 98308
  242.1 0.6 copy-start.18

commit v2 on v1

--- a/solution.py
+++ b/solution.py
@@ -17,13 +17,13 @@
 EPS = 1e-05
 C = 0.125 * 1.4426950408889634
 T_LOW, T_HIGH = 2.0 ** -60, 2.0 ** 100
-TQ = 512
-VMEM_LIMIT = 56 * 2 ** 20
+TQ = 1024
+VMEM_LIMIT = 24 * 2 ** 20
 NAMES = ("ylo", "z", "x", "yhi", "core")
-YC = ("ylo", "yhi", "core")
 VM = pl.BlockSpec(memory_space=pltpu.VMEM)
 SM = pl.BlockSpec(memory_space=pltpu.SMEM)
 ANY = pl.BlockSpec(memory_space=pl.ANY)
+HBM = pl.BlockSpec(memory_space=pltpu.HBM)
 
 
 def call(kernel, ins, specs, outs, scratch=(), us=2):
@@ -71,14 +71,17 @@
     return rows[0:1] + rows[1:2] + rows[2:3], rows[3:4] + rows[4:5] + rows[5:6]
 
 
-def project_kernel(pos, own, sib, gain, wq, wk, wv, m0, m1, m2, m3, wbuf, sems):
+def project_kernel(pos, own_hbm, sib, gain_hbm, wq, wk, wv, m0, m1, m2, m3, own, gain, wbuf, sems):
     y, core = pos[0], pos[1]
     cols = pl.ds(pl.multiple_of(core * 256, 256), 256)
+    first = [pltpu.make_async_copy(own_hbm, own, sems.at[3]), pltpu.make_async_copy(gain_hbm, gain, sems.at[4])]
     copies = [
         pltpu.make_async_copy(w.at[:, cols], wbuf.at[i], sems.at[i]) for i, w in enumerate((wk, wv, wq))
     ]
-    for copy in copies:
+    for copy in first + copies:
         copy.start()
+    for copy in first:
+        copy.wait()
     g = gain[...]
     normed = jnp.concatenate(
         [norm_rows(own[...], g).astype(BF), norm_rows(sib[...], g).astype(BF)], axis=0
@@ -158,13 +161,13 @@
     return acc
 
 
-def exact(q_ref, chunks, kv_s, acc_ref, top_ref):
+def exact(q_ref, chunks, kv_s, acc_ref, top_ref, start):
     for i, ref in enumerate(chunks):
         pltpu.sync_copy(ref, kv_s.at[i])
 
     def tile(t, carry):
         cols = pl.ds(pl.multiple_of(t * 256, 256), 256)
-        q = q_ref[0:64, cols]
+        q = q_ref[0:64, pl.ds(pl.multiple_of(start + t * 256, 256), 256)]
 
         def chunk(i, state):
             acc, old = state
@@ -183,36 +186,37 @@
         top_ref[:, cols] = jnp.broadcast_to(top, (8, 256))
         return carry
 
-    lax.fori_loop(0, q_ref.shape[1] // 256, tile, 0)
-
-
-def finish(q_ref, chunks, kv_s, acc_ref, top_ref):
+    lax.fori_loop(0, acc_ref.shape[1] // 256, tile, 0)
+
+
+def finish(q_ref, chunks, kv_s, acc_ref, top_ref, start=0):
     total = acc_ref[0:1, :]
     fits = jnp.where((total >= T_LOW) & (total <= T_HIGH), 1.0, 0.0)
 
     @pl.when(jnp.min(fits) < 0.5)
     def _():
-        exact(q_ref, chunks, kv_s, acc_ref, top_ref)
-
-
-def tiles_of(q_ref, acc_in, chunks, acc_ref, top_ref):
+        exact(q_ref, chunks, kv_s, acc_ref, top_ref, start)
+
+
+def tiles_of(q_ref, acc_in, chunks, acc_ref, top_ref, start=0, size=TQ, count=None):
     def tile(t, carry):
-        cols = pl.ds(pl.multiple_of(t * TQ, TQ), TQ)
-        rhs, shift = augmented(q_ref[0:64, cols], q_ref[64:80, cols])
+        from_cols = pl.ds(pl.multiple_of(start + t * size, 256), size)
+        cols = pl.ds(pl.multiple_of(t * size, 256), size)
+        rhs, shift = augmented(q_ref[0:64, from_cols], q_ref[64:80, from_cols])
         if acc_in is None:
-            acc = jnp.zeros((128, TQ), F32)
+            acc = jnp.zeros((128, size), F32)
         else:
-            rows = acc_in[:, cols]
-            acc = jnp.concatenate([jnp.broadcast_to(rows[0:1], (56, TQ)), rows], axis=0)
+            rows = acc_in[:, from_cols]
+            acc = jnp.concatenate([jnp.broadcast_to(rows[0:1], (56, size)), rows], axis=0)
         acc = attend(rhs, chunks, acc)
         if top_ref is None:
             acc_ref[:, cols] = acc[56:128]
         else:
             acc_ref[:, cols] = acc
-            top_ref[:, cols] = jnp.broadcast_to(shift, (8, TQ))
+            top_ref[:, cols] = jnp.broadcast_to(shift, (8, size))
         return carry
 
-    lax.fori_loop(0, q_ref.shape[1] // TQ, tile, 0)
+    lax.fori_loop(0, q_ref.shape[1] // size if count is None else count, tile, 0)
 
 
 def gather_queries(qs, q_s):
@@ -247,77 +251,117 @@
         out[64:80, :] = stats_rows(acc_s[0:1, cols], top_s[0:1, cols])
 
 
-def own_kernel(count, *refs):
-    qx, own_kv = refs[0], refs[1]
-    chunks = list(refs[2:2 + count])
+def own_sums(qx, own_kv, chunks, acc_in, acc_s, top_s, kv_s, start, size):
+    tiles_of(qx, acc_in, chunks, acc_s, top_s, start, size, 1)
+    finish(qx, [own_kv] + chunks, kv_s, acc_s, top_s, start)
+
+
+def others_kernel(count, *refs):
     acc_in, out, acc_s, top_s, kv_s = refs[2 + count:]
-    tiles_of(qx, acc_in, chunks, acc_s, top_s)
-    finish(qx, [own_kv] + chunks, kv_s, acc_s, top_s)
+    own_sums(refs[0], refs[1], list(refs[2:2 + count]), acc_in, acc_s, top_s, kv_s, 256, 768)
     out[0:64, :] = acc_s[64:128, :]
-    out[64:72, :] = jnp.broadcast_to(acc_s[0:1, :], (8, GRP))
+    out[64:72, :] = jnp.broadcast_to(acc_s[0:1, :], (8, 768))
     out[72:80, :] = top_s[...]
 
 
-def combine_kernel(pos, own, r1, r2, r3, out):
-    y, core = pos[0], pos[1]
-    sums = [own[0:64, :]] + [r[0:64, :].astype(F32) for r in (r1, r2, r3)]
-    stats = [(own[64:65, :], own[72:73, :])] + [stats_read(r[64:80, :]) for r in (r1, r2, r3)]
+def context_of(sums, total, top, received, cols):
+    sums = [sums] + [r[0:64, cols].astype(F32) for r in received]
+    stats = [(total, top)] + [stats_read(r[64:80, cols]) for r in received]
     top = functools.reduce(jnp.maximum, [s[1] for s in stats])
     factors = [jnp.exp2((s[1] - top) * C) for s in stats]
     total = sum(f * s[0] for f, s in zip(factors, stats))
-    context = (sum(f * s for f, s in zip(factors, sums)) / total).astype(BF)
-    for i in range(4):
-        to_y = lax.rem(y + 4 - i, 4)
-        for j in range(2):
-            to_core = core if j == 0 else 1 - core
-            to = lax.rem(to_y, 2) * 4 + lax.div(to_y, 2) * 2 + to_core
-            out[to] = context[:, (2 * i + j) * 128:(2 * i + j + 1) * 128]
-
-
-def expand_kernel(ctx, frames, w_out, gain, w_expand, hidden, glu, head, tail, wo, we, sems):
-    copies = [pltpu.make_async_copy(w_out, wo, sems.at[0])]
-    for i in range(4):
-        block = i % 2 * 1024 + i // 2 * 512
-        copies.append(pltpu.make_async_copy(
-            w_expand.at[:, block:block + 512], we.at[:, block:block + 512], sems.at[1 + i]))
-    for copy in copies:
-        copy.start()
-    order = [yy % 2 * 4 + yy // 2 * 2 + cc for cc in range(2) for yy in range(4)]
-    context = jnp.concatenate([ctx[s] for s in order], axis=0).T
-    copies[0].wait()
-    h = (frames[...].astype(F32) + mm(context, wo[...])).astype(BF)
+    return (sum(f * s for f, s in zip(factors, sums)) / total).astype(BF)
+
+
+def combine_kernel(part, r1, r2, r3, c1, c2, c3):
+    context = context_of(part[0:64, :], part[64:65, :], part[72:73, :], (r1, r2, r3), slice(256, 1024))
+    for i, out in enumerate((c1, c2, c3)):
+        out[0:64, :] = context[:, i * 256:i * 256 + 128]
+        out[64:128, :] = context[:, i * 256 + 128:(i + 1) * 256]
+
+
+def here_kernel(count, *refs):
+    acc_in, r1, r2, r3, out, acc_s, top_s, kv_s = refs[2 + count:]
+    own_sums(refs[0], refs[1], list(refs[2:2 + count]), acc_in, acc_s, top_s, kv_s, 0, 256)
+    context = context_of(acc_s[64:128, :], acc_s[0:1, :], top_s[0:1, :], (r1, r2, r3), slice(0, 256))
+    out[0:64, :] = context[:, 0:128]
+    out[64:128, :] = context[:, 128:256]
+
+
+def sibling_kernel(c0, c1, c2, c3, out):
+    for i, c in enumerate((c0, c1, c2, c3)):
+        out[i * 64:(i + 1) * 64, :] = c[64:128, :]
+
+
+def expand_kernel(pos, c0, c1, c2, c3, theirs, frames, w_out, gain, w_expand, hidden, glu, inner, outer, ctx):
+    y, core = pos[0], pos[1]
+    for i, c in enumerate((c0, c1, c2, c3)):
+        head = lax.rem(y + i, 4)
+        ctx[pl.ds(pl.multiple_of((core * 4 + head) * 64, 64), 64), :] = c[0:64, :]
+        ctx[pl.ds(pl.multiple_of(((1 - core) * 4 + head) * 64, 64), 64), :] = theirs[i * 64:(i + 1) * 64, :]
+    context = ctx[...].T
+    h = (frames[...].astype(F32) + mm(context, w_out[...])).astype(BF)
     hidden[...] = h
     normed = norm_rows(h, gain[...]).astype(BF)
     for i in range(2):
-        copies[1 + 2 * i].wait()
-        value = mm(normed, we[:, i * 512:(i + 1) * 512])
-        copies[2 + 2 * i].wait()
-        gate = mm(normed, we[:, 1024 + i * 512:1024 + (i + 1) * 512])
+        value = mm(normed, w_expand[:, i * 512:(i + 1) * 512])
+        gate = mm(normed, w_expand[:, 1024 + i * 512:1024 + (i + 1) * 512])
         g = (value * jax.nn.sigmoid(gate)).astype(BF)
         cols = slice(i * 512, (i + 1) * 512)
         glu[:, cols] = g
-        head[:, cols] = g[:16]
-        tail[:, cols] = g[OWN - 16:]
-
-
-def conv_kernel(before, glu, after, hidden, taps, scale, shift, w_project, out, pad, act, wp, sem):
-    copy = pltpu.make_async_copy(w_project, wp, sem)
-    copy.start()
-    pad[0:16, :] = before[...].astype(F32)
-    pad[16:16 + OWN, :] = glu[...].astype(F32)
-    pad[16 + OWN:32 + OWN, :] = after[...].astype(F32)
+
+    @pl.when(core == 0)
+    def _():
+        inner[...] = glu[OWN - 16:, :]
+        outer[...] = glu[:16, :]
+
+    @pl.when(core == 1)
+    def _():
+        inner[...] = glu[:16, :]
+        outer[...] = glu[OWN - 16:, :]
+
+
+def conv_kernel(glu, taps, conv, pad):
+    for i in range(8):
+        pad[i, 0:16, :] = jnp.zeros((16, 128), F32)
+        pad[i, 16:16 + OWN, :] = glu[:, i * 128:(i + 1) * 128].astype(F32)
+        pad[i, 16 + OWN:32 + OWN, :] = jnp.zeros((16, 128), F32)
 
     def block(i, carry):
         cols = pl.ds(pl.multiple_of(i * 128, 128), 128)
-        conv = jnp.zeros((OWN, 128), F32)
+        total = jnp.zeros((OWN, 128), F32)
         for tap in range(31):
-            conv = conv + taps[tap:tap + 1, cols] * pad[1 + tap:1 + tap + OWN, cols]
-        act[:, cols] = jax.nn.silu(scale[:, cols] * conv + shift[:, cols]).astype(BF)
+            total = total + taps[tap:tap + 1, cols] * pad[i, 1 + tap:1 + tap + OWN, :]
+        conv[:, cols] = total
         return carry
 
     lax.fori_loop(0, D // 128, block, 0)
-    copy.wait()
-    out[...] = (hidden[...].astype(F32) + mm(act[...], wp[...])).astype(BF)
+
+
+def close_kernel(pos, conv, inner, outer, hidden, taps, scale, shift, w_project, out, edge):
+    core = pos[1]
+    first = jnp.where(core == 0, 1.0, 0.0)
+    for i in range(8):
+        cols = slice(i * 128, (i + 1) * 128)
+        one, two = inner[:, cols].astype(F32), outer[:, cols].astype(F32)
+        before = first * two + (1.0 - first) * one
+        after = first * one + (1.0 - first) * two
+        edge[i, 0:16, :] = before
+        edge[i, 16:32, :] = jnp.zeros((16, 128), F32)
+        edge[i, 32:48, :] = after
+    parts = []
+    for i in range(8):
+        cols = slice(i * 128, (i + 1) * 128)
+        top = conv[0:16, cols]
+        low = conv[OWN - 16:OWN, cols]
+        for tap in range(15):
+            top = top + taps[tap:tap + 1, cols] * edge[i, 1 + tap:17 + tap, :]
+            late = 16 + tap
+            low = low + taps[late:late + 1, cols] * edge[i, 1 + late:17 + late, :]
+        total = jnp.concatenate([top, conv[16:OWN - 16, cols], low], axis=0)
+        parts.append(jax.nn.silu(scale[:, cols] * total + shift[:, cols]).astype(BF))
+    act = jnp.concatenate(parts, axis=1)
+    out[...] = (hidden[...].astype(F32) + mm(act, w_project[...])).astype(BF)
 
 
 def body(frames, gain_attn, w_query, w_key, w_value, w_out, gain_conv, w_expand, kernel_taps, bn_scale, bn_shift, w_project):
@@ -334,22 +378,27 @@
         return lax.ppermute(value, ("ylo", "yhi"), [(place_of(i), place_of((i + step) % 4)) for i in range(4)])
 
     row = lambda v: v.reshape(1, -1)
+    stay = lambda v: pltpu.with_memory_space_constraint(v, pltpu.HBM)
     sib = along("core", frames, 1)
     sent = call(
-        project_kernel, (pos, frames, sib, row(gain_attn), w_query, w_key, w_value), [SM, VM, VM, VM, ANY, ANY, ANY],
-        [((384, 128), BF)] * 4, [pltpu.VMEM((3, D, 256), BF), pltpu.SemaphoreType.DMA((3,))],
+        project_kernel, (pos, stay(frames), sib, stay(row(gain_attn)), stay(w_query), stay(w_key), stay(w_value)),
+        [SM, HBM, VM, HBM, HBM, HBM, HBM], [((384, 128), BF)] * 4,
+        [pltpu.VMEM((OWN, D), BF), pltpu.VMEM((1, D), F32), pltpu.VMEM((3, D, 256), BF), pltpu.SemaphoreType.DMA((5,))],
     )
     got = [sent[0]] + [along_y(sent[i], i) for i in (1, 2, 3)]
     kv, qx = call(pack_kernel, got, [VM] * 4, [((GRP, 128), BF), ((80, GRP), BF)])
     up1, down1 = along("z", kv, 1), along("z", kv, -1)
     queries = [along("x", qx, i) for i in (1, 2, 3)]
     own_acc, = call(start_kernel, (qx, kv), [VM] * 2, [((72, GRP), F32)], us=2)
-    up1, down1, own_acc = lax.optimization_barrier((up1, down1, own_acc))
-    up2, down2 = along("z", up1, 1), along("z", down1, -1)
     many = ((72, 3 * GRP), F32)
     q_scratch = pltpu.VMEM((80, 3 * GRP), BF)
     acc, = call(
-        functools.partial(remote_kernel, 3, True, False), (*queries, kv, up1, down1), [VM] * 6, [many], [q_scratch], us=10,
+        functools.partial(remote_kernel, 1, True, False), (*queries, kv), [VM] * 4, [many], [q_scratch], us=3,
+    )
+    up1, down1, own_acc, acc = lax.optimization_barrier((up1, down1, own_acc, acc))
+    up2, down2 = along("z", up1, 1), along("z", down1, -1)
+    acc, = call(
+        functools.partial(remote_kernel, 2, False, False), (*queries, up1, down1, acc), [VM] * 6, [many], [q_scratch], us=7,
     )
     up2, down2, acc = lax.optimization_barrier((up2, down2, acc))
     up3, down3 = along("z", up2, 1), along("z", down2, -1)
@@ -370,24 +419,32 @@
     )
     returned = [along("x", parts[i - 1], -i) for i in (1, 2, 3)]
     chunks = (up1, down1, up2, down2, up3, down3, up4)
-    own_part, = call(
-        functools.partial(own_kernel, 7), (qx, kv, *chunks, own_acc), [VM] * 10, [((80, GRP), F32)],
-        [pltpu.VMEM((128, GRP), F32), pltpu.VMEM((8, GRP), F32), pltpu.VMEM((8, GRP, 128), BF)], us=8,
-    )
-    contexts, = call(combine_kernel, (pos, own_part, *returned), [SM] + [VM] * 4, [((8, HD, 128), BF)])
-    contexts = lax.all_to_all(contexts, YC, 0, 0)
-    hidden, glu, head, tail = call(
-        expand_kernel, (contexts, frames, w_out, row(gain_conv), w_expand), [VM, VM, ANY, VM, ANY],
-        [((OWN, D), BF), ((OWN, D), BF), ((16, D), BF), ((16, D), BF)],
-        [pltpu.VMEM((512, D), BF), pltpu.VMEM((D, 2 * D), BF), pltpu.SemaphoreType.DMA((5,))],
+    scratch = lambda n: [pltpu.VMEM((128, n), F32), pltpu.VMEM((8, n), F32), pltpu.VMEM((8, GRP, 128), BF)]
+    part, = call(
+        functools.partial(others_kernel, 7), (qx, kv, *chunks, own_acc), [VM] * 10, [((80, 768), F32)], scratch(768), us=6,
+    )
+    away = call(combine_kernel, (part, *returned), [VM] * 4, [((128, 128), BF)] * 3, us=1)
+    home = [along_y(away[i - 1], -i) for i in (1, 2, 3)]
+    here, = call(
+        functools.partial(here_kernel, 7), (qx, kv, *chunks, own_acc, *returned), [VM] * 13, [((128, 128), BF)],
+        scratch(256), us=3,
+    )
+    contexts = [here] + home
+    theirs, = call(sibling_kernel, contexts, [VM] * 4, [((256, 128), BF)], us=1)
+    theirs = along("core", theirs, 1)
+    hidden, glu, inner, outer = call(
+        expand_kernel, (pos, *contexts, theirs, frames, w_out, row(gain_conv), w_expand), [SM] + [VM] * 9,
+        [((OWN, D), BF), ((OWN, D), BF), ((16, D), BF), ((16, D), BF)], [pltpu.VMEM((512, 128), BF)], us=2,
     )
     count = lax.axis_size(NAMES)
-    before = lax.ppermute(tail, NAMES, [(i, i + 1) for i in range(count - 1)])
-    after = lax.ppermute(head, NAMES, [(i + 1, i) for i in range(count - 1)])
+    outer = lax.ppermute(
+        outer, NAMES, [(i, i - 1) for i in range(2, count, 2)] + [(i, i + 1) for i in range(1, count - 1, 2)]
+    )
+    inner = along("core", inner, 1)
+    conv, = call(conv_kernel, (glu, kernel_taps), [VM] * 2, [((OWN, D), F32)], [pltpu.VMEM((8, OWN + 32, 128), F32)], us=3)
     out, = call(
-        conv_kernel, (before, glu, after, hidden, kernel_taps, row(bn_scale), row(bn_shift), w_project),
-        [VM] * 7 + [ANY], [((OWN, D), BF)],
-        [pltpu.VMEM((OWN + 32, D), F32), pltpu.VMEM((OWN, D), BF), pltpu.VMEM((D, D), BF), pltpu.SemaphoreType.DMA],
+        close_kernel, (pos, conv, inner, outer, hidden, kernel_taps, row(bn_scale), row(bn_shift), w_project),
+        [SM] + [VM] * 8, [((OWN, D), BF)], [pltpu.VMEM((8, 48, 128), F32)], us=2,
     )
     return out
 

time: 249 us -> 208 us (0.84)
  Pallas kernels: 187 us -> 156 us
  blocking collectives: 13.6 us -> 0 us
  starting transfers between devices: 27.7 us -> 37.5 us
  local copies, waits for them, and re-layouts: 5.34 us -> 0.04 us
    pallas_call x11 -> x15, Pallas kernels: 187 us -> 156 us  [call(): pl.pallas_call(kernel, in_specs=specs, out_specs=[VM] * len(outs), out_sh...]
    all_to_all x1 -> x0, blocking collectives: 13.6 us -> none  [body(): contexts = lax.all_to_all(contexts, YC, 0, 0)]
    ppermute x14 -> x16, starting transfers between devices: 18.9 us -> 28.7 us  [along(): lax.ppermute(value, axis, [(i, (i + step) % count) for i in range(count)])]
    unnamed x38 -> x16, local copies, waits for them, and re-layouts: 5.34 us -> 0.04 us
    ppermute x2 -> x1, waiting for transfers between devices: 5 us -> 1.59 us  [body(): lax.ppermute(outer, NAMES, [(i, i - 1) for i in range(2, count, 2)] + [(i...]
    ppermute x14 -> x16, waiting for transfers between devices: 4.47 us -> 6.71 us  [along(): lax.ppermute(value, axis, [(i, (i + step) % count) for i in range(count)])]
    ppermute x2 -> x1, starting transfers between devices: 5.48 us -> 3.86 us  [body(): lax.ppermute(outer, NAMES, [(i, i - 1) for i in range(2, count, 2)] + [(i...]
  transfers between devices with their start and end apart: 19 -> 23, of which waited for: 7 -> 8; matrix products, arithmetic and copies ran while one was open for 0% -> 0% of each run, Pallas kernels for 28% -> 28%
where the time goes in v2:
time: 208 us; the launch traced here: 206 us
  Pallas kernels  156 us (75%)
  starting transfers between devices  37.5 us (18%)
  waiting for transfers between devices  12.6 us (6%)
    pallas_call x15, Pallas kernels, call(): pl.pallas_call(kernel, in_specs=specs, out_specs=[VM] * len(outs), out_sh...  156 us
    ppermute x16, starting transfers between devices, along(): lax.ppermute(value, axis, [(i, (i + step) % count) for i in range(count)])  28.7 us
    ppermute x16, waiting for transfers between devices, along(): lax.ppermute(value, axis, [(i, (i + step) % count) for i in range(count)])  6.71 us
    ppermute x6, starting transfers between devices, along_y(): lax.ppermute(value, ('ylo', 'yhi'), [(place_of(i), place_of((i + step) %...  4.95 us
    ppermute x6, waiting for transfers between devices, along_y(): lax.ppermute(value, ('ylo', 'yhi'), [(place_of(i), place_of((i + step) %...  4.34 us
  transfers between devices with their start and end apart: 23, of which 8 were waited for; matrix products, arithmetic and copies ran while one was open for 0% of the time, Pallas kernels for 28%

profile of v2, /device:TPU:1, one launch (start us, length us, event | category | flops | bytes accessed | tf_op | source)
XLA Modules:
  0.0 206.1 jit_solution(6125801394119443801)
XLA Ops:
  0.0 3.2 %collective-permute-start = (bf16[128,1024]{1,0:T(8,128)(2,1)}, bf16[128,1024]{1,0:T(8,128)(2,1)S(1)}, u32[]{:S(2)}, u32[]{:S(2)}) collective-permute-start(bf16[128,1024]{1,0:T(8,128)(2,1)} %frames.1), channel_id=1, source_target_pairs={{0,1},{1,0},{2,3},{3,2},{4,5},{5,4},{6,7},{7,6},{8,9},{9,8},{10,11... | collective-permute-start | bytes 786440 | tf_op jit(solution)/shard_map/ppermute | solution.py:374
  3.2 0.1 pad_add_fusion.pos
  3.3 1.3 collective-permute-done.sib
  4.6 3.2 %shard_map.118 = (bf16[384,128]{1,0:T(8,128)(2,1)S(1)}, bf16[384,128]{1,0:T(8,128)(2,1)S(1)}, bf16[384,128]{1,0:T(8,128)(2,1)S(1)}, bf16[384,128]{1,0:T(8,128)(2,1)S(1)}) custom-call(s32[2]{0:T(128)S(1)} %pad_add_fusion.pos, bf16[128,1024]{1,0:T(8,128)(2,1)} %frames.1, bf16[128,1024]{1,0:T(8,128)(2,1)S(1)} %collective-permute-done.sib, f32[1,1024]{1,0:T(1,128)} %bitcast.9, ...), custom_call_target="tpu_custom_call" | custom-call | flops 2000000000 | bytes 1024 | tf_op jit(solution)/shard_map/pallas_call | solution.py:30
  7.8 0.1 collective-permute-start.1
  7.9 2.2 %collective-permute-start.2 = (bf16[384,128]{1,0:T(8,128)(2,1)S(1)}, bf16[384,128]{1,0:T(8,128)(2,1)S(1)}, u32[]{:S(2)}, u32[]{:S(2)}) collective-permute-start(bf16[384,128]{1,0:T(8,128)(2,1)S(1)} %get-tuple-element.33), channel_id=1, source_target_pairs={{0,2},{128,130},{2,0},{130,128},{1,3},{129,131},{3,1},{131,129},{4... | collective-permute-start | bytes 294920 | tf_op jit(solution)/shard_map/ppermute | solution.py:378
  10.1 1.1 collective-permute-start.3
  11.2 2.5 %collective-permute-done.1.a1 = bf16[384,128]{1,0:T(8,128)(2,1)S(1)} collective-permute-done((bf16[384,128]{1,0:T(8,128)(2,1)S(1)}, bf16[384,128]{1,0:T(8,128)(2,1)S(1)}, u32[]{:S(2)}, u32[]{:S(2)}) %collective-permute-start.1) | collective-permute-done | bytes 98336 | tf_op jit(solution)/shard_map/ppermute | solution.py:378
  13.7 1.1 collective-permute-done.2.a2
  14.8 0.8 collective-permute-done.3.a3
  15.5 0.4 shard_map.119
  16.0 1.8 collective-permute-start.8
  17.8 0.5 collective-permute-start.7
  18.3 0.6 collective-permute-start.6
  18.9 5.6 %collective-permute-start.5 = (bf16[1024,128]{1,0:T(8,128)(2,1)S(1)}, bf16[1024,128]{1,0:T(8,128)(2,1)S(1)}, u32[]{:S(2)}, u32[]{:S(2)}) collective-permute-start(bf16[1024,128]{1,0:T(8,128)(2,1)S(1)} %get-tuple-element.36.kv.refs_3_.refs_4_.refs_1_), channel_id=1, source_target_pairs={{0,112},{16,0},{32,16},{48,32},{64,48},{80,64},{96,80},{112,96},{1... | collective-permute-start | bytes 786440 | tf_op jit(solution)/shard_map/ppermute | solution.py:374
  24.5 1.0 shard_map.120.refs_9_
  25.5 3.0 %collective-permute-done.6.refs_0_ = bf16[80,1024]{1,0:T(8,128)(2,1)S(1)} collective-permute-done((bf16[80,1024]{1,0:T(8,128)(2,1)S(1)}, bf16[80,1024]{1,0:T(8,128)(2,1)S(1)}, u32[]{:S(2)}, u32[]{:S(2)}) %collective-permute-start.6) | collective-permute-done | bytes 163872 | tf_op jit(solution)/shard_map/ppermute | solution.py:374
  28.5 3.1 %shard_map.121.refs_5_ = f32[72,3072]{1,0:T(8,128)S(1)} custom-call(bf16[80,1024]{1,0:T(8,128)(2,1)S(1)} %collective-permute-done.6.refs_0_, bf16[80,1024]{1,0:T(8,128)(2,1)S(1)} %collective-permute-done.7.refs_1_, bf16[80,1024]{1,0:T(8,128)(2,1)S(1)} %collective-permute-done.8.refs_2_, bf16[1024,128]{1,0:T(8,128)(2,1)S(1)} %get-tuple-element.36.kv.refs_3_.refs_4_.refs_1_), custom_call_target="tpu_custom_call" | custom-call | flops 3000000000 | bytes 1024 | tf_op jit(solution)/shard_map/pallas_call | solution.py:30
  31.6 1.7 collective-permute-start.9
  33.3 4.2 %collective-permute-start.10 = (bf16[1024,128]{1,0:T(8,128)(2,1)S(1)}, bf16[1024,128]{1,0:T(8,128)(2,1)S(1)}, u32[]{:S(2)}, u32[]{:S(2)}) collective-permute-start(bf16[1024,128]{1,0:T(8,128)(2,1)S(1)} %collective-permute-done.5.refs_4_.refs_6_.refs_3_), channel_id=1, source_target_pairs={{0,112},{16,0},{32,16},{48,32},{64,48},{80,64},{96,80},{112,96},{1... | collective-permute-start | bytes 786440 | tf_op jit(solution)/shard_map/ppermute | solution.py:374
  37.5 5.5 %shard_map.122.refs_5_ = f32[72,3072]{1,0:T(8,128)S(1)} custom-call(bf16[80,1024]{1,0:T(8,128)(2,1)S(1)} %collective-permute-done.6.refs_0_, bf16[80,1024]{1,0:T(8,128)(2,1)S(1)} %collective-permute-done.7.refs_1_, bf16[80,1024]{1,0:T(8,128)(2,1)S(1)} %collective-permute-done.8.refs_2_, bf16[1024,128]{1,0:T(8,128)(2,1)S(1)} %collective-permute-done.4.refs_3_.refs_5_.refs_2_, ...), custom_call_target="tpu_custom_call" | custom-call | flops 7000000000 | bytes 1024 | tf_op jit(solution)/shard_map/pallas_call | solution.py:30
  43.0 0.1 collective-permute-start.11
  43.1 2.7 %collective-permute-start.12 = (bf16[1024,128]{1,0:T(8,128)(2,1)S(1)}, bf16[1024,128]{1,0:T(8,128)(2,1)S(1)}, u32[]{:S(2)}, u32[]{:S(2)}) collective-permute-start(bf16[1024,128]{1,0:T(8,128)(2,1)S(1)} %collective-permute-done.10.refs_4_.refs_8_.refs_5_), channel_id=1, source_target_pairs={{0,112},{16,0},{32,16},{48,32},{64,48},{80,64},{96,80},{112,96},{1... | collective-permute-start | bytes 786440 | tf_op jit(solution)/shard_map/ppermute | solution.py:374
  45.7 5.5 %shard_map.123.refs_5_ = f32[72,3072]{1,0:T(8,128)S(1)} custom-call(bf16[80,1024]{1,0:T(8,128)(2,1)S(1)} %collective-permute-done.6.refs_0_, bf16[80,1024]{1,0:T(8,128)(2,1)S(1)} %collective-permute-done.7.refs_1_, bf16[80,1024]{1,0:T(8,128)(2,1)S(1)} %collective-permute-done.8.refs_2_, bf16[1024,128]{1,0:T(8,128)(2,1)S(1)} %collective-permute-done.9.refs_3_.refs_7_.refs_4_, ...), custom_call_target="tpu_custom_call" | custom-call | flops 7000000000 | bytes 1024 | tf_op jit(solution)/shard_map/pallas_call | solution.py:30
  51.3 0.1 collective-permute-start.13
  51.4 5.5 %shard_map.124.refs_11_ = f32[72,3072]{1,0:T(8,128)S(1)} custom-call(bf16[80,1024]{1,0:T(8,128)(2,1)S(1)} %collective-permute-done.6.refs_0_, bf16[80,1024]{1,0:T(8,128)(2,1)S(1)} %collective-permute-done.7.refs_1_, bf16[80,1024]{1,0:T(8,128)(2,1)S(1)} %collective-permute-done.8.refs_2_, ...), custom_call_target="tpu_custom_call" | custom-call | flops 7000000000 | bytes 1024 | tf_op jit(solution)/shard_map/pallas_call | solution.py:30
  56.8 1.5 collective-permute-done.13.refs_3_.refs_8_
  58.4 90.2 %shard_map.125 = (bf16[80,1024]{1,0:T(8,128)(2,1)S(1)}, bf16[80,1024]{1,0:T(8,128)(2,1)S(1)}, bf16[80,1024]{1,0:T(8,128)(2,1)S(1)}) custom-call(bf16[80,1024]{1,0:T(8,128)(2,1)S(1)} %collective-permute-done.6.refs_0_, bf16[80,1024]{1,0:T(8,128)(2,1)S(1)} %collective-permute-done.7.refs_1_, bf16[80,1024]{1,0:T(8,128)(2,1)S(1)} %collective-permute-done.8.refs_2_, ...), custom_call_target="tpu_custom_call" | custom-call | flops 4000000000 | bytes 1024 | tf_op jit(solution)/shard_map/pallas_call | solution.py:30
  148.6 0.1 collective-permute-start.14
  148.7 0.1 collective-permute-start.15
  148.8 1.4 collective-permute-start.16
  150.2 26.6 %shard_map.127.part = f32[80,768]{1,0:T(8,128)S(1)} custom-call(bf16[80,1024]{1,0:T(8,128)(2,1)S(1)} %get-tuple-element.35.qx.refs_0_, bf16[1024,128]{1,0:T(8,128)(2,1)S(1)} %get-tuple-element.36.kv.refs_3_.refs_4_.refs_1_, bf16[1024,128]{1,0:T(8,128)(2,1)S(1)} %collective-permute-done.4.refs_3_.refs_5_.refs_2_, ...), custom_call_target="tpu_custom_call" | custom-call | flops 6000000000 | bytes 1024 | tf_op jit(solution)/shard_map/pallas_call | solution.py:30
  176.8 0.1 shard_map.128
  176.9 0.2 collective-permute-start.17
  177.1 0.9 collective-permute-start.18
  178.0 0.5 collective-permute-start.19
  178.5 9.4 %shard_map.126.c0 = bf16[128,128]{1,0:T(8,128)(2,1)S(1)} custom-call(bf16[80,1024]{1,0:T(8,128)(2,1)S(1)} %get-tuple-element.35.qx.refs_0_, bf16[1024,128]{1,0:T(8,128)(2,1)S(1)} %get-tuple-element.36.kv.refs_3_.refs_4_.refs_1_, bf16[1024,128]{1,0:T(8,128)(2,1)S(1)} %collective-permute-done.4.refs_3_.refs_5_.refs_2_, ...), custom_call_target="tpu_custom_call" | custom-call | flops 3000000000 | bytes 1024 | tf_op jit(solution)/shard_map/pallas_call | solution.py:30
  187.9 0.0 copy-start.4
  188.0 6.2 %collective-permute-start.20 = (bf16[256,128]{1,0:T(8,128)(2,1)S(1)}, bf16[256,128]{1,0:T(8,128)(2,1)S(1)}, u32[]{:S(2)}, u32[]{:S(2)}) collective-permute-start(bf16[256,128]{1,0:T(8,128)(2,1)S(1)} %shard_map.129), channel_id=1, source_target_pairs={{0,1},{1,0},{2,3},{3,2},{4,5},{5,4},{6,7},{7,6},{8,9},{9,8},{10,11... | collective-permute-start | bytes 196616 | tf_op jit(solution)/shard_map/ppermute | solution.py:374
  194.2 0.9 collective-permute-done.20.theirs
  195.1 1.8 shard_map.130
  196.9 0.4 collective-permute-start.21
  197.4 3.9 %collective-permute-start.22 = (bf16[16,1024]{1,0:T(8,128)(2,1)S(1)}, bf16[16,1024]{1,0:T(8,128)(2,1)S(1)}, u32[]{:S(2)}, u32[]{:S(2)}) collective-permute-start(bf16[16,1024]{1,0:T(8,128)(2,1)S(1)} %get-tuple-element.55), channel_id=1, source_target_pairs={{2,1},{4,3},{6,5},{8,7},{10,9},{12,11},{14,13},{16,15},{18,17},{20... | collective-permute-start | bytes 98312 | tf_op jit(solution)/shard_map/ppermute | solution.py:440
  201.3 0.0 copy-start.6
  201.3 0.0 copy-start.7
  201.3 1.2 shard_map.131.conv
  202.5 1.6 collective-permute-done.22.outer
  204.1 2.0 shard_map.132
  (30 shorter events, 0.1 us)
Async XLA Ops:
  0.0 4.6 %collective-permute-start = (bf16[128,1024]{1,0:T(8,128)(2,1)}, bf16[128,1024]{1,0:T(8,128)(2,1)S(1)}, u32[]{:S(2)}, u32[]{:S(2)}) collective-permute-start(bf16[128,1024]{1,0:T(8,128)(2,1)} %frames.1), channel_id=1, source_target_pairs={{0,1},{1,0},{2,3},{3,2},{4,5},{5,4},{6,7},{7,6},{8,9},{9,8},{10,11... | collective-permute-start | bytes 786440 | tf_op jit(solution)/shard_map/ppermute | solution.py:374
  7.8 5.8 %collective-permute-start.1 = (bf16[384,128]{1,0:T(8,128)(2,1)S(1)}, bf16[384,128]{1,0:T(8,128)(2,1)S(1)}, u32[]{:S(2)}, u32[]{:S(2)}) collective-permute-start(bf16[384,128]{1,0:T(8,128)(2,1)S(1)} %get-tuple-element.32), channel_id=1, source_target_pairs={{0,128},{128,2},{2,130},{130,0},{1,129},{129,3},{3,131},{131,1},{4... | collective-permute-start | bytes 294920 | tf_op jit(solution)/shard_map/ppermute | solution.py:378
  7.9 6.8 %collective-permute-start.2 = (bf16[384,128]{1,0:T(8,128)(2,1)S(1)}, bf16[384,128]{1,0:T(8,128)(2,1)S(1)}, u32[]{:S(2)}, u32[]{:S(2)}) collective-permute-start(bf16[384,128]{1,0:T(8,128)(2,1)S(1)} %get-tuple-element.33), channel_id=1, source_target_pairs={{0,2},{128,130},{2,0},{130,128},{1,3},{129,131},{3,1},{131,129},{4... | collective-permute-start | bytes 294920 | tf_op jit(solution)/shard_map/ppermute | solution.py:378
  10.1 5.4 %collective-permute-start.3 = (bf16[384,128]{1,0:T(8,128)(2,1)S(1)}, bf16[384,128]{1,0:T(8,128)(2,1)S(1)}, u32[]{:S(2)}, u32[]{:S(2)}) collective-permute-start(bf16[384,128]{1,0:T(8,128)(2,1)S(1)} %get-tuple-element.34), channel_id=1, source_target_pairs={{0,130},{128,0},{2,128},{130,2},{1,131},{129,1},{3,129},{131,3},{4... | collective-permute-start | bytes 294920 | tf_op jit(solution)/shard_map/ppermute | solution.py:378
  16.0 9.5 %collective-permute-start.8 = (bf16[80,1024]{1,0:T(8,128)(2,1)S(1)}, bf16[80,1024]{1,0:T(8,128)(2,1)S(1)}, u32[]{:S(2)}, u32[]{:S(2)}) collective-permute-start(bf16[80,1024]{1,0:T(8,128)(2,1)S(1)} %get-tuple-element.35.qx.refs_0_), channel_id=1, source_target_pairs={{0,12},{4,0},{8,4},{12,8},{1,13},{5,1},{9,5},{13,9},{2,14},{6,2},{... | collective-permute-start | bytes 491528 | tf_op jit(solution)/shard_map/ppermute | solution.py:374
  17.8 7.7 %collective-permute-start.7 = (bf16[80,1024]{1,0:T(8,128)(2,1)S(1)}, bf16[80,1024]{1,0:T(8,128)(2,1)S(1)}, u32[]{:S(2)}, u32[]{:S(2)}) collective-permute-start(bf16[80,1024]{1,0:T(8,128)(2,1)S(1)} %get-tuple-element.35.qx.refs_0_), channel_id=1, source_target_pairs={{0,8},{4,12},{8,0},{12,4},{1,9},{5,13},{9,1},{13,5},{2,10},{6,14},... | collective-permute-start | bytes 491528 | tf_op jit(solution)/shard_map/ppermute | solution.py:374
  18.3 10.2 %collective-permute-start.6 = (bf16[80,1024]{1,0:T(8,128)(2,1)S(1)}, bf16[80,1024]{1,0:T(8,128)(2,1)S(1)}, u32[]{:S(2)}, u32[]{:S(2)}) collective-permute-start(bf16[80,1024]{1,0:T(8,128)(2,1)S(1)} %get-tuple-element.35.qx.refs_0_), channel_id=1, source_target_pairs={{0,4},{4,8},{8,12},{12,0},{1,5},{5,9},{9,13},{13,1},{2,6},{6,10},{... | collective-permute-start | bytes 491528 | tf_op jit(solution)/shard_map/ppermute | solution.py:374
  18.9 12.7 %collective-permute-start.5 = (bf16[1024,128]{1,0:T(8,128)(2,1)S(1)}, bf16[1024,128]{1,0:T(8,128)(2,1)S(1)}, u32[]{:S(2)}, u32[]{:S(2)}) collective-permute-start(bf16[1024,128]{1,0:T(8,128)(2,1)S(1)} %get-tuple-element.36.kv.refs_3_.refs_4_.refs_1_), channel_id=1, source_target_pairs={{0,112},{16,0},{32,16},{48,32},{64,48},{80,64},{96,80},{112,96},{1... | collective-permute-start | bytes 786440 | tf_op jit(solution)/shard_map/ppermute | solution.py:374
  24.5 7.1 %collective-permute-start.4 = (bf16[1024,128]{1,0:T(8,128)(2,1)S(1)}, bf16[1024,128]{1,0:T(8,128)(2,1)S(1)}, u32[]{:S(2)}, u32[]{:S(2)}) collective-permute-start(bf16[1024,128]{1,0:T(8,128)(2,1)S(1)} %get-tuple-element.36.kv.refs_3_.refs_4_.refs_1_), channel_id=1, source_target_pairs={{0,16},{16,32},{32,48},{48,64},{64,80},{80,96},{96,112},{112,0},{1... | collective-permute-start | bytes 786440 | tf_op jit(solution)/shard_map/ppermute | solution.py:374
  31.6 11.4 %collective-permute-start.9 = (bf16[1024,128]{1,0:T(8,128)(2,1)S(1)}, bf16[1024,128]{1,0:T(8,128)(2,1)S(1)}, u32[]{:S(2)}, u32[]{:S(2)}) collective-permute-start(bf16[1024,128]{1,0:T(8,128)(2,1)S(1)} %collective-permute-done.4.refs_3_.refs_5_.refs_2_), channel_id=1, source_target_pairs={{0,16},{16,32},{32,48},{48,64},{64,80},{80,96},{96,112},{112,0},{1... | collective-permute-start | bytes 786440 | tf_op jit(solution)/shard_map/ppermute | solution.py:374
  33.3 9.7 %collective-permute-start.10 = (bf16[1024,128]{1,0:T(8,128)(2,1)S(1)}, bf16[1024,128]{1,0:T(8,128)(2,1)S(1)}, u32[]{:S(2)}, u32[]{:S(2)}) collective-permute-start(bf16[1024,128]{1,0:T(8,128)(2,1)S(1)} %collective-permute-done.5.refs_4_.refs_6_.refs_3_), channel_id=1, source_target_pairs={{0,112},{16,0},{32,16},{48,32},{64,48},{80,64},{96,80},{112,96},{1... | collective-permute-start | bytes 786440 | tf_op jit(solution)/shard_map/ppermute | solution.py:374
  43.0 8.2 %collective-permute-start.11 = (bf16[1024,128]{1,0:T(8,128)(2,1)S(1)}, bf16[1024,128]{1,0:T(8,128)(2,1)S(1)}, u32[]{:S(2)}, u32[]{:S(2)}) collective-permute-start(bf16[1024,128]{1,0:T(8,128)(2,1)S(1)} %collective-permute-done.9.refs_3_.refs_7_.refs_4_), channel_id=1, source_target_pairs={{0,16},{16,32},{32,48},{48,64},{64,80},{80,96},{96,112},{112,0},{1... | collective-permute-start | bytes 786440 | tf_op jit(solution)/shard_map/ppermute | solution.py:374
  43.1 8.2 %collective-permute-start.12 = (bf16[1024,128]{1,0:T(8,128)(2,1)S(1)}, bf16[1024,128]{1,0:T(8,128)(2,1)S(1)}, u32[]{:S(2)}, u32[]{:S(2)}) collective-permute-start(bf16[1024,128]{1,0:T(8,128)(2,1)S(1)} %collective-permute-done.10.refs_4_.refs_8_.refs_5_), channel_id=1, source_target_pairs={{0,112},{16,0},{32,16},{48,32},{64,48},{80,64},{96,80},{112,96},{1... | collective-permute-start | bytes 786440 | tf_op jit(solution)/shard_map/ppermute | solution.py:374
  51.3 7.1 %collective-permute-start.13 = (bf16[1024,128]{1,0:T(8,128)(2,1)S(1)}, bf16[1024,128]{1,0:T(8,128)(2,1)S(1)}, u32[]{:S(2)}, u32[]{:S(2)}) collective-permute-start(bf16[1024,128]{1,0:T(8,128)(2,1)S(1)} %collective-permute-done.11.refs_3_.refs_9_.refs_6_), channel_id=1, source_target_pairs={{0,16},{16,32},{32,48},{48,64},{64,80},{80,96},{96,112},{112,0},{1... | collective-permute-start | bytes 786440 | tf_op jit(solution)/shard_map/ppermute | solution.py:374
  148.6 28.1 %collective-permute-start.14 = (bf16[80,1024]{1,0:T(8,128)(2,1)S(1)}, bf16[80,1024]{1,0:T(8,128)(2,1)S(1)}, u32[]{:S(2)}, u32[]{:S(2)}) collective-permute-start(bf16[80,1024]{1,0:T(8,128)(2,1)S(1)} %get-tuple-element.47), channel_id=1, source_target_pairs={{0,12},{4,0},{8,4},{12,8},{1,13},{5,1},{9,5},{13,9},{2,14},{6,2},{... | collective-permute-start | bytes 491528 | tf_op jit(solution)/shard_map/ppermute | solution.py:374
  148.7 28.0 %collective-permute-start.15 = (bf16[80,1024]{1,0:T(8,128)(2,1)S(1)}, bf16[80,1024]{1,0:T(8,128)(2,1)S(1)}, u32[]{:S(2)}, u32[]{:S(2)}) collective-permute-start(bf16[80,1024]{1,0:T(8,128)(2,1)S(1)} %get-tuple-element.48), channel_id=1, source_target_pairs={{0,8},{4,12},{8,0},{12,4},{1,9},{5,13},{9,1},{13,5},{2,10},{6,14},... | collective-permute-start | bytes 491528 | tf_op jit(solution)/shard_map/ppermute | solution.py:374
  148.8 27.9 %collective-permute-start.16 = (bf16[80,1024]{1,0:T(8,128)(2,1)S(1)}, bf16[80,1024]{1,0:T(8,128)(2,1)S(1)}, u32[]{:S(2)}, u32[]{:S(2)}) collective-permute-start(bf16[80,1024]{1,0:T(8,128)(2,1)S(1)} %get-tuple-element.49), channel_id=1, source_target_pairs={{0,4},{4,8},{8,12},{12,0},{1,5},{5,9},{9,13},{13,1},{2,6},{6,10},{... | collective-permute-start | bytes 491528 | tf_op jit(solution)/shard_map/ppermute | solution.py:374
  176.9 11.0 %collective-permute-start.17 = (bf16[128,128]{1,0:T(8,128)(2,1)S(1)}, bf16[128,128]{1,0:T(8,128)(2,1)S(1)}, u32[]{:S(2)}, u32[]{:S(2)}) collective-permute-start(bf16[128,128]{1,0:T(8,128)(2,1)S(1)} %get-tuple-element.50), channel_id=1, source_target_pairs={{0,130},{128,0},{2,128},{130,2},{1,131},{129,1},{3,129},{131,3},{4... | collective-permute-start | bytes 98312 | tf_op jit(solution)/shard_map/ppermute | solution.py:378
  177.1 10.8 %collective-permute-start.18 = (bf16[128,128]{1,0:T(8,128)(2,1)S(1)}, bf16[128,128]{1,0:T(8,128)(2,1)S(1)}, u32[]{:S(2)}, u32[]{:S(2)}) collective-permute-start(bf16[128,128]{1,0:T(8,128)(2,1)S(1)} %get-tuple-element.51), channel_id=1, source_target_pairs={{0,2},{128,130},{2,0},{130,128},{1,3},{129,131},{3,1},{131,129},{4... | collective-permute-start | bytes 98312 | tf_op jit(solution)/shard_map/ppermute | solution.py:378
  178.0 17.0 %copy-start = (bf16[1024,2048]{1,0:T(8,128)(2,1)S(1)}, bf16[1024,2048]{1,0:T(8,128)(2,1)}, u32[]{:S(2)}) copy-start(bf16[1024,2048]{1,0:T(8,128)(2,1)} %w_expand.1) | copy-start | bytes 12582916
  178.0 17.0 %copy-start.2 = (bf16[512,1024]{1,0:T(8,128)(2,1)S(1)}, bf16[512,1024]{1,0:T(8,128)(2,1)}, u32[]{:S(2)}) copy-start(bf16[512,1024]{1,0:T(8,128)(2,1)} %w_out.1) | copy-start | bytes 3145732
  178.0 17.0 %copy-start.3 = (bf16[128,1024]{1,0:T(8,128)(2,1)S(1)}, bf16[128,1024]{1,0:T(8,128)(2,1)}, u32[]{:S(2)}) copy-start(bf16[128,1024]{1,0:T(8,128)(2,1)} %frames.1) | copy-start | bytes 786436
  178.0 17.0 %copy-start.5 = (f32[1024]{0:T(1024)S(1)}, f32[1024]{0:T(1024)}, u32[]{:S(2)}) copy-start(f32[1024]{0:T(1024)} %param.18) | copy-start | bytes 12292
  178.0 9.9 %collective-permute-start.19 = (bf16[128,128]{1,0:T(8,128)(2,1)S(1)}, bf16[128,128]{1,0:T(8,128)(2,1)S(1)}, u32[]{:S(2)}, u32[]{:S(2)}) collective-permute-start(bf16[128,128]{1,0:T(8,128)(2,1)S(1)} %get-tuple-element.52), channel_id=1, source_target_pairs={{0,128},{128,2},{2,130},{130,0},{1,129},{129,3},{3,131},{131,1},{4... | collective-permute-start | bytes 98312 | tf_op jit(solution)/shard_map/ppermute | solution.py:378
  187.9 13.3 %copy-start.4 = (f32[31,1024]{1,0:T(8,128)S(1)}, f32[31,1024]{1,0:T(8,128)}, u32[]{:S(2)}) copy-start(f32[31,1024]{1,0:T(8,128)} %taps.3) | copy-start | bytes 380932
  188.0 7.1 %collective-permute-start.20 = (bf16[256,128]{1,0:T(8,128)(2,1)S(1)}, bf16[256,128]{1,0:T(8,128)(2,1)S(1)}, u32[]{:S(2)}, u32[]{:S(2)}) collective-permute-start(bf16[256,128]{1,0:T(8,128)(2,1)S(1)} %shard_map.129), channel_id=1, source_target_pairs={{0,1},{1,0},{2,3},{3,2},{4,5},{5,4},{6,7},{7,6},{8,9},{9,8},{10,11... | collective-permute-start | bytes 196616 | tf_op jit(solution)/shard_map/ppermute | solution.py:374
  196.9 5.6 %collective-permute-start.21 = (bf16[16,1024]{1,0:T(8,128)(2,1)S(1)}, bf16[16,1024]{1,0:T(8,128)(2,1)S(1)}, u32[]{:S(2)}, u32[]{:S(2)}) collective-permute-start(bf16[16,1024]{1,0:T(8,128)(2,1)S(1)} %get-tuple-element.54), channel_id=1, source_target_pairs={{0,1},{1,0},{2,3},{3,2},{4,5},{5,4},{6,7},{7,6},{8,9},{9,8},{10,11... | collective-permute-start | bytes 98312 | tf_op jit(solution)/shard_map/ppermute | solution.py:374
  197.4 6.7 %collective-permute-start.22 = (bf16[16,1024]{1,0:T(8,128)(2,1)S(1)}, bf16[16,1024]{1,0:T(8,128)(2,1)S(1)}, u32[]{:S(2)}, u32[]{:S(2)}) collective-permute-start(bf16[16,1024]{1,0:T(8,128)(2,1)S(1)} %get-tuple-element.55), channel_id=1, source_target_pairs={{2,1},{4,3},{6,5},{8,7},{10,9},{12,11},{14,13},{16,15},{18,17},{20... | collective-permute-start | bytes 98312 | tf_op jit(solution)/shard_map/ppermute | solution.py:440
  201.3 2.8 %copy-start.1 = (bf16[1024,1024]{1,0:T(8,128)(2,1)S(1)}, bf16[1024,1024]{1,0:T(8,128)(2,1)}, u32[]{:S(2)}) copy-start(bf16[1024,1024]{1,0:T(8,128)(2,1)} %w_project.1) | copy-start | bytes 6291460
  201.3 2.8 %copy-start.6 = (f32[1024]{0:T(1024)S(1)}, f32[1024]{0:T(1024)}, u32[]{:S(2)}) copy-start(f32[1024]{0:T(1024)} %param.21) | copy-start | bytes 12292
  201.3 2.8 %copy-start.7 = (f32[1024]{0:T(1024)S(1)}, f32[1024]{0:T(1024)}, u32[]{:S(2)}) copy-start(f32[1024]{0:T(1024)} %param.22) | copy-start | bytes 12292

commit v3 on v2

--- a/solution.py
+++ b/solution.py
@@ -71,26 +71,24 @@
     return rows[0:1] + rows[1:2] + rows[2:3], rows[3:4] + rows[4:5] + rows[5:6]
 
 
-def project_kernel(pos, own_hbm, sib, gain_hbm, wq, wk, wv, m0, m1, m2, m3, own, gain, wbuf, sems):
-    y, core = pos[0], pos[1]
-    cols = pl.ds(pl.multiple_of(core * 256, 256), 256)
+def fetch_kernel(pos, own_hbm, gain_hbm, wq, wk, wv, w, normed, gain, own, sems):
+    cols = pl.ds(pl.multiple_of(pos[1] * 256, 256), 256)
     first = [pltpu.make_async_copy(own_hbm, own, sems.at[3]), pltpu.make_async_copy(gain_hbm, gain, sems.at[4])]
-    copies = [
-        pltpu.make_async_copy(w.at[:, cols], wbuf.at[i], sems.at[i]) for i, w in enumerate((wk, wv, wq))
-    ]
+    copies = [pltpu.make_async_copy(v.at[:, cols], w.at[i], sems.at[i]) for i, v in enumerate((wk, wv, wq))]
     for copy in first + copies:
         copy.start()
     for copy in first:
         copy.wait()
-    g = gain[...]
-    normed = jnp.concatenate(
-        [norm_rows(own[...], g).astype(BF), norm_rows(sib[...], g).astype(BF)], axis=0
-    )
-    copies[0].wait()
+    normed[...] = norm_rows(own[...], gain[...]).astype(BF)
+    for copy in copies:
+        copy.wait()
+
+
+def project_kernel(pos, own, sib, gain, wbuf, m0, m1, m2, m3):
+    y = pos[0]
+    normed = jnp.concatenate([own[...], norm_rows(sib[...], gain[...]).astype(BF)], axis=0)
     k = mm(normed, wbuf[0])
-    copies[1].wait()
     vt = mm(normed, wbuf[1]).T.astype(BF)
-    copies[2].wait()
     qt = mm(normed, wbuf[2]).T.astype(BF)
     blocks = []
     for h in range(4):
@@ -226,6 +224,20 @@
 
 def start_kernel(qx, kv, acc):
     tiles_of(qx, None, [kv], acc, None)
+
+
+def first_kernel(count, *refs):
+    acc, q_s = refs[count + 1:]
+    for t in range(count):
+        q_s[:, t * GRP:(t + 1) * GRP] = refs[t][...]
+    tiles_of(q_s, None, [refs[count]], acc, None)
+
+
+def second_kernel(q1, q2, q3, up, down, acc_near, acc_far, acc, q_s, acc_s):
+    gather_queries((q1, q2, q3), q_s)
+    acc_s[:, 0:2 * GRP] = acc_near[...]
+    acc_s[:, 2 * GRP:3 * GRP] = acc_far[...]
+    tiles_of(q_s, acc_s, [up, down], acc, None)
 
 
 def remote_kernel(count, first, last, *refs):
@@ -380,11 +392,12 @@
     row = lambda v: v.reshape(1, -1)
     stay = lambda v: pltpu.with_memory_space_constraint(v, pltpu.HBM)
     sib = along("core", frames, 1)
-    sent = call(
-        project_kernel, (pos, stay(frames), sib, stay(row(gain_attn)), stay(w_query), stay(w_key), stay(w_value)),
-        [SM, HBM, VM, HBM, HBM, HBM, HBM], [((384, 128), BF)] * 4,
-        [pltpu.VMEM((OWN, D), BF), pltpu.VMEM((1, D), F32), pltpu.VMEM((3, D, 256), BF), pltpu.SemaphoreType.DMA((5,))],
-    )
+    weights, normed, gain = call(
+        fetch_kernel, (pos, stay(frames), stay(row(gain_attn)), stay(w_query), stay(w_key), stay(w_value)),
+        [SM, HBM, HBM, HBM, HBM, HBM], [((3, D, 256), BF), ((OWN, D), BF), ((1, D), F32)],
+        [pltpu.VMEM((OWN, D), BF), pltpu.SemaphoreType.DMA((5,))], us=2,
+    )
+    sent = call(project_kernel, (pos, normed, sib, gain, weights), [SM] + [VM] * 4, [((384, 128), BF)] * 4)
     got = [sent[0]] + [along_y(sent[i], i) for i in (1, 2, 3)]
     kv, qx = call(pack_kernel, got, [VM] * 4, [((GRP, 128), BF), ((80, GRP), BF)])
     up1, down1 = along("z", kv, 1), along("z", kv, -1)
@@ -392,13 +405,20 @@
     own_acc, = call(start_kernel, (qx, kv), [VM] * 2, [((72, GRP), F32)], us=2)
     many = ((72, 3 * GRP), F32)
     q_scratch = pltpu.VMEM((80, 3 * GRP), BF)
-    acc, = call(
-        functools.partial(remote_kernel, 1, True, False), (*queries, kv), [VM] * 4, [many], [q_scratch], us=3,
-    )
-    up1, down1, own_acc, acc = lax.optimization_barrier((up1, down1, own_acc, acc))
+    order = (1, 3, 2)
+    queries = [queries[i - 1] for i in order]
+    acc_near, = call(
+        functools.partial(first_kernel, 2), (*queries[:2], kv), [VM] * 3, [((72, 2 * GRP), F32)],
+        [pltpu.VMEM((80, 2 * GRP), BF)], us=2,
+    )
+    acc_far, = call(
+        functools.partial(first_kernel, 1), (queries[2], kv), [VM] * 2, [((72, GRP), F32)], [pltpu.VMEM((80, GRP), BF)], us=1,
+    )
+    up1, down1, own_acc, acc_near, acc_far = lax.optimization_barrier((up1, down1, own_acc, acc_near, acc_far))
     up2, down2 = along("z", up1, 1), along("z", down1, -1)
     acc, = call(
-        functools.partial(remote_kernel, 2, False, False), (*queries, up1, down1, acc), [VM] * 6, [many], [q_scratch], us=7,
+        second_kernel, (*queries, up1, down1, acc_near, acc_far), [VM] * 7, [many],
+        [q_scratch, pltpu.VMEM((72, 3 * GRP), F32)], us=7,
     )
     up2, down2, acc = lax.optimization_barrier((up2, down2, acc))
     up3, down3 = along("z", up2, 1), along("z", down2, -1)
@@ -417,7 +437,7 @@
         [q_scratch, pltpu.VMEM((128, 3 * GRP), F32), pltpu.VMEM((8, 3 * GRP), F32), pltpu.VMEM((8, GRP, 128), BF)],
         us=4,
     )
-    returned = [along("x", parts[i - 1], -i) for i in (1, 2, 3)]
+    returned = [along("x", part, -i) for i, part in zip(order, parts)]
     chunks = (up1, down1, up2, down2, up3, down3, up4)
     scratch = lambda n: [pltpu.VMEM((128, n), F32), pltpu.VMEM((8, n), F32), pltpu.VMEM((8, GRP, 128), BF)]
     part, = call(
@@ -440,8 +460,9 @@
     outer = lax.ppermute(
         outer, NAMES, [(i, i - 1) for i in range(2, count, 2)] + [(i, i + 1) for i in range(1, count - 1, 2)]
     )
+    conv, = call(conv_kernel, (glu, kernel_taps), [VM] * 2, [((OWN, D), F32)], [pltpu.VMEM((8, OWN + 32, 128), F32)], us=3)
+    inner, conv = lax.optimization_barrier((inner, conv))
     inner = along("core", inner, 1)
-    conv, = call(conv_kernel, (glu, kernel_taps), [VM] * 2, [((OWN, D), F32)], [pltpu.VMEM((8, OWN + 32, 128), F32)], us=3)
     out, = call(
         close_kernel, (pos, conv, inner, outer, hidden, kernel_taps, row(bn_scale), row(bn_shift), w_project),
         [SM] + [VM] * 8, [((OWN, D), BF)], [pltpu.VMEM((8, 48, 128), F32)], us=2,

time: 208 us -> 207 us (level)
    pallas_call x15 -> x17, Pallas kernels: 156 us -> 156 us  [call(): pl.pallas_call(kernel, in_specs=specs, out_specs=[VM] * len(outs), out_sh...]
  transfers between devices with their start and end apart: 23 -> 23, of which waited for: 8 -> 7; matrix products, arithmetic and copies ran while one was open for 0% -> 0% of each run, Pallas kernels for 28% -> 29%
where the time goes in v3:
time: 207 us; the launch traced here: 206 us
  Pallas kernels  156 us (75%)
  starting transfers between devices  38.6 us (19%)
  waiting for transfers between devices  10.8 us (5%)
    pallas_call x17, Pallas kernels, call(): pl.pallas_call(kernel, in_specs=specs, out_specs=[VM] * len(outs), out_sh...  156 us
    ppermute x16, starting transfers between devices, along(): lax.ppermute(value, axis, [(i, (i + step) % count) for i in range(count)])  28.7 us
    ppermute x6, starting transfers between devices, along_y(): lax.ppermute(value, ('ylo', 'yhi'), [(place_of(i), place_of((i + step) %...  5.53 us
    ppermute x16, waiting for transfers between devices, along(): lax.ppermute(value, axis, [(i, (i + step) % count) for i in range(count)])  5.02 us
    ppermute x6, waiting for transfers between devices, along_y(): lax.ppermute(value, ('ylo', 'yhi'), [(place_of(i), place_of((i + step) %...  4.76 us
    ppermute x1, starting transfers between devices, body(): lax.ppermute(outer, NAMES, [(i, i - 1) for i in range(2, count, 2)] + [(i...  4.38 us
  transfers between devices with their start and end apart: 23, of which 7 were waited for; matrix products, arithmetic and copies ran while one was open for 0% of the time, Pallas kernels for 29%

profile of v3, /device:TPU:1, one launch (start us, length us, event | category | flops | bytes accessed | tf_op | source)
XLA Modules:
  0.0 205.7 jit_solution(17844510273922212134)
XLA Ops:
  0.0 3.2 %collective-permute-start = (bf16[128,1024]{1,0:T(8,128)(2,1)}, bf16[128,1024]{1,0:T(8,128)(2,1)S(1)}, u32[]{:S(2)}, u32[]{:S(2)}) collective-permute-start(bf16[128,1024]{1,0:T(8,128)(2,1)} %frames.1), channel_id=1, source_target_pairs={{0,1},{1,0},{2,3},{3,2},{4,5},{5,4},{6,7},{7,6},{8,9},{9,8},{10,11... | collective-permute-start | bytes 786440 | tf_op jit(solution)/shard_map/ppermute | solution.py:386
  3.2 0.1 pad_add_fusion.pos
  3.3 2.0 shard_map.118
  5.4 1.4 shard_map.119
  6.8 0.1 collective-permute-start.1
  6.9 2.2 %collective-permute-start.2 = (bf16[384,128]{1,0:T(8,128)(2,1)S(1)}, bf16[384,128]{1,0:T(8,128)(2,1)S(1)}, u32[]{:S(2)}, u32[]{:S(2)}) collective-permute-start(bf16[384,128]{1,0:T(8,128)(2,1)S(1)} %get-tuple-element.42), channel_id=1, source_target_pairs={{0,2},{128,130},{2,0},{130,128},{1,3},{129,131},{3,1},{131,129},{4... | collective-permute-start | bytes 294920 | tf_op jit(solution)/shard_map/ppermute | solution.py:390
  9.1 1.1 collective-permute-start.3
  10.2 4.5 %collective-permute-done.1.a1 = bf16[384,128]{1,0:T(8,128)(2,1)S(1)} collective-permute-done((bf16[384,128]{1,0:T(8,128)(2,1)S(1)}, bf16[384,128]{1,0:T(8,128)(2,1)S(1)}, u32[]{:S(2)}, u32[]{:S(2)}) %collective-permute-start.1) | collective-permute-done | bytes 98336 | tf_op jit(solution)/shard_map/ppermute | solution.py:390
  14.7 0.3 collective-permute-done.3.a3
  14.9 0.4 shard_map.120
  15.4 2.1 %collective-permute-start.8 = (bf16[80,1024]{1,0:T(8,128)(2,1)S(1)}, bf16[80,1024]{1,0:T(8,128)(2,1)S(1)}, u32[]{:S(2)}, u32[]{:S(2)}) collective-permute-start(bf16[80,1024]{1,0:T(8,128)(2,1)S(1)} %get-tuple-element.44.qx.refs_0_), channel_id=1, source_target_pairs={{0,8},{4,12},{8,0},{12,4},{1,9},{5,13},{9,1},{13,5},{2,10},{6,14},... | collective-permute-start | bytes 491528 | tf_op jit(solution)/shard_map/ppermute | solution.py:386
  17.4 0.9 collective-permute-start.7
  18.3 0.6 collective-permute-start.6
  18.9 5.6 %collective-permute-start.5 = (bf16[1024,128]{1,0:T(8,128)(2,1)S(1)}, bf16[1024,128]{1,0:T(8,128)(2,1)S(1)}, u32[]{:S(2)}, u32[]{:S(2)}) collective-permute-start(bf16[1024,128]{1,0:T(8,128)(2,1)S(1)} %get-tuple-element.45.kv.refs_2_.refs_1_.refs_4_), channel_id=1, source_target_pairs={{0,112},{16,0},{32,16},{48,32},{64,48},{80,64},{96,80},{112,96},{1... | collective-permute-start | bytes 786440 | tf_op jit(solution)/shard_map/ppermute | solution.py:386
  24.5 1.0 shard_map.121.refs_9_
  25.5 1.0 shard_map.123.acc_far
  26.5 2.1 shard_map.122.acc_near
  28.6 3.0 %collective-permute-done.4.up.refs_5_.refs_2_ = bf16[1024,128]{1,0:T(8,128)(2,1)S(1)} collective-permute-done((bf16[1024,128]{1,0:T(8,128)(2,1)S(1)}, bf16[1024,128]{1,0:T(8,128)(2,1)S(1)}, u32[]{:S(2)}, u32[]{:S(2)}) %collective-permute-start.4) | collective-permute-done | bytes 262176 | tf_op jit(solution)/shard_map/ppermute | solution.py:386
  31.6 2.7 %collective-permute-start.10 = (bf16[1024,128]{1,0:T(8,128)(2,1)S(1)}, bf16[1024,128]{1,0:T(8,128)(2,1)S(1)}, u32[]{:S(2)}, u32[]{:S(2)}) collective-permute-start(bf16[1024,128]{1,0:T(8,128)(2,1)S(1)} %collective-permute-done.5.down.refs_6_.refs_3_), channel_id=1, source_target_pairs={{0,112},{16,0},{32,16},{48,32},{64,48},{80,64},{96,80},{112,96},{1... | collective-permute-start | bytes 786440 | tf_op jit(solution)/shard_map/ppermute | solution.py:386
  34.3 5.5 %shard_map.124.refs_5_ = f32[72,3072]{1,0:T(8,128)S(1)} custom-call(bf16[80,1024]{1,0:T(8,128)(2,1)S(1)} %collective-permute-done.6.refs_0_.q1, bf16[80,1024]{1,0:T(8,128)(2,1)S(1)} %collective-permute-done.7.refs_1_.q2, bf16[80,1024]{1,0:T(8,128)(2,1)S(1)} %collective-permute-done.8.refs_0_.q3.refs_2_, ...), custom_call_target="tpu_custom_call" | custom-call | flops 7000000000 | bytes 1024 | tf_op jit(solution)/shard_map/pallas_call | solution.py:30
  39.8 0.1 collective-permute-start.11
  39.9 2.7 %collective-permute-start.12 = (bf16[1024,128]{1,0:T(8,128)(2,1)S(1)}, bf16[1024,128]{1,0:T(8,128)(2,1)S(1)}, u32[]{:S(2)}, u32[]{:S(2)}) collective-permute-start(bf16[1024,128]{1,0:T(8,128)(2,1)S(1)} %collective-permute-done.10.refs_4_.refs_8_.refs_5_), channel_id=1, source_target_pairs={{0,112},{16,0},{32,16},{48,32},{64,48},{80,64},{96,80},{112,96},{1... | collective-permute-start | bytes 786440 | tf_op jit(solution)/shard_map/ppermute | solution.py:386
  42.6 5.5 %shard_map.125.refs_5_ = f32[72,3072]{1,0:T(8,128)S(1)} custom-call(bf16[80,1024]{1,0:T(8,128)(2,1)S(1)} %collective-permute-done.6.refs_0_.q1, bf16[80,1024]{1,0:T(8,128)(2,1)S(1)} %collective-permute-done.7.refs_1_.q2, bf16[80,1024]{1,0:T(8,128)(2,1)S(1)} %collective-permute-done.8.refs_0_.q3.refs_2_, ...), custom_call_target="tpu_custom_call" | custom-call | flops 7000000000 | bytes 1024 | tf_op jit(solution)/shard_map/pallas_call | solution.py:30
  48.1 0.1 collective-permute-start.13
  48.2 5.5 %shard_map.126.refs_11_ = f32[72,3072]{1,0:T(8,128)S(1)} custom-call(bf16[80,1024]{1,0:T(8,128)(2,1)S(1)} %collective-permute-done.6.refs_0_.q1, bf16[80,1024]{1,0:T(8,128)(2,1)S(1)} %collective-permute-done.7.refs_1_.q2, bf16[80,1024]{1,0:T(8,128)(2,1)S(1)} %collective-permute-done.8.refs_0_.q3.refs_2_, ...), custom_call_target="tpu_custom_call" | custom-call | flops 7000000000 | bytes 1024 | tf_op jit(solution)/shard_map/pallas_call | solution.py:30
  53.7 0.9 collective-permute-done.13.refs_3_.refs_8_
  54.6 90.2 %shard_map.127 = (bf16[80,1024]{1,0:T(8,128)(2,1)S(1)}, bf16[80,1024]{1,0:T(8,128)(2,1)S(1)}, bf16[80,1024]{1,0:T(8,128)(2,1)S(1)}) custom-call(bf16[80,1024]{1,0:T(8,128)(2,1)S(1)} %collective-permute-done.6.refs_0_.q1, bf16[80,1024]{1,0:T(8,128)(2,1)S(1)} %collective-permute-done.7.refs_1_.q2, ...), custom_call_target="tpu_custom_call" | custom-call | flops 4000000000 | bytes 1024 | tf_op jit(solution)/shard_map/pallas_call | solution.py:30
  144.8 2.2 %collective-permute-start.14 = (bf16[80,1024]{1,0:T(8,128)(2,1)S(1)}, bf16[80,1024]{1,0:T(8,128)(2,1)S(1)}, u32[]{:S(2)}, u32[]{:S(2)}) collective-permute-start(bf16[80,1024]{1,0:T(8,128)(2,1)S(1)} %get-tuple-element.57), channel_id=1, source_target_pairs={{0,12},{4,0},{8,4},{12,8},{1,13},{5,1},{9,5},{13,9},{2,14},{6,2},{... | collective-permute-start | bytes 491528 | tf_op jit(solution)/shard_map/ppermute | solution.py:386
  147.0 2.0 collective-permute-start.16
  149.0 26.6 %shard_map.129.part = f32[80,768]{1,0:T(8,128)S(1)} custom-call(bf16[80,1024]{1,0:T(8,128)(2,1)S(1)} %get-tuple-element.44.qx.refs_0_, bf16[1024,128]{1,0:T(8,128)(2,1)S(1)} %get-tuple-element.45.kv.refs_2_.refs_1_.refs_4_, bf16[1024,128]{1,0:T(8,128)(2,1)S(1)} %collective-permute-done.4.up.refs_5_.refs_2_, ...), custom_call_target="tpu_custom_call" | custom-call | flops 6000000000 | bytes 1024 | tf_op jit(solution)/shard_map/pallas_call | solution.py:30
  175.6 0.1 shard_map.130
  175.7 0.8 collective-permute-start.17
  176.5 0.6 collective-permute-start.18
  177.2 0.8 collective-permute-start.19
  178.0 9.4 %shard_map.128.c0 = bf16[128,128]{1,0:T(8,128)(2,1)S(1)} custom-call(bf16[80,1024]{1,0:T(8,128)(2,1)S(1)} %get-tuple-element.44.qx.refs_0_, bf16[1024,128]{1,0:T(8,128)(2,1)S(1)} %get-tuple-element.45.kv.refs_2_.refs_1_.refs_4_, bf16[1024,128]{1,0:T(8,128)(2,1)S(1)} %collective-permute-done.4.up.refs_5_.refs_2_, ...), custom_call_target="tpu_custom_call" | custom-call | flops 3000000000 | bytes 1024 | tf_op jit(solution)/shard_map/pallas_call | solution.py:30
  187.3 0.0 copy-start.2
  187.3 0.0 copy-start.3
  187.3 0.0 copy-start.5
  187.4 6.5 %collective-permute-start.20 = (bf16[256,128]{1,0:T(8,128)(2,1)S(1)}, bf16[256,128]{1,0:T(8,128)(2,1)S(1)}, u32[]{:S(2)}, u32[]{:S(2)}) collective-permute-start(bf16[256,128]{1,0:T(8,128)(2,1)S(1)} %shard_map.131), channel_id=1, source_target_pairs={{0,1},{1,0},{2,3},{3,2},{4,5},{5,4},{6,7},{7,6},{8,9},{9,8},{10,11... | collective-permute-start | bytes 196616 | tf_op jit(solution)/shard_map/ppermute | solution.py:386
  193.9 0.9 collective-permute-done.20.theirs
  194.9 1.8 shard_map.132
  196.7 4.4 %collective-permute-start.22 = (bf16[16,1024]{1,0:T(8,128)(2,1)S(1)}, bf16[16,1024]{1,0:T(8,128)(2,1)S(1)}, u32[]{:S(2)}, u32[]{:S(2)}) collective-permute-start(bf16[16,1024]{1,0:T(8,128)(2,1)S(1)} %get-tuple-element.67), channel_id=1, source_target_pairs={{2,1},{4,3},{6,5},{8,7},{10,9},{12,11},{14,13},{16,15},{18,17},{20... | collective-permute-start | bytes 98312 | tf_op jit(solution)/shard_map/ppermute | solution.py:460
  201.1 0.0 copy-start.1
  201.1 1.2 shard_map.133.conv
  202.3 0.1 collective-permute-start.21
  202.4 1.0 collective-permute-done.22.outer
  203.4 0.2 collective-permute-done.21.inner
  203.6 2.0 shard_map.134
  (32 shorter events, 0.1 us)
Async XLA Ops:
  0.0 5.4 %collective-permute-start = (bf16[128,1024]{1,0:T(8,128)(2,1)}, bf16[128,1024]{1,0:T(8,128)(2,1)S(1)}, u32[]{:S(2)}, u32[]{:S(2)}) collective-permute-start(bf16[128,1024]{1,0:T(8,128)(2,1)} %frames.1), channel_id=1, source_target_pairs={{0,1},{1,0},{2,3},{3,2},{4,5},{5,4},{6,7},{7,6},{8,9},{9,8},{10,11... | collective-permute-start | bytes 786440 | tf_op jit(solution)/shard_map/ppermute | solution.py:386
  6.8 7.8 %collective-permute-start.1 = (bf16[384,128]{1,0:T(8,128)(2,1)S(1)}, bf16[384,128]{1,0:T(8,128)(2,1)S(1)}, u32[]{:S(2)}, u32[]{:S(2)}) collective-permute-start(bf16[384,128]{1,0:T(8,128)(2,1)S(1)} %get-tuple-element.41), channel_id=1, source_target_pairs={{0,128},{128,2},{2,130},{130,0},{1,129},{129,3},{3,131},{131,1},{4... | collective-permute-start | bytes 294920 | tf_op jit(solution)/shard_map/ppermute | solution.py:390
  6.9 7.7 %collective-permute-start.2 = (bf16[384,128]{1,0:T(8,128)(2,1)S(1)}, bf16[384,128]{1,0:T(8,128)(2,1)S(1)}, u32[]{:S(2)}, u32[]{:S(2)}) collective-permute-start(bf16[384,128]{1,0:T(8,128)(2,1)S(1)} %get-tuple-element.42), channel_id=1, source_target_pairs={{0,2},{128,130},{2,0},{130,128},{1,3},{129,131},{3,1},{131,129},{4... | collective-permute-start | bytes 294920 | tf_op jit(solution)/shard_map/ppermute | solution.py:390
  9.1 5.8 %collective-permute-start.3 = (bf16[384,128]{1,0:T(8,128)(2,1)S(1)}, bf16[384,128]{1,0:T(8,128)(2,1)S(1)}, u32[]{:S(2)}, u32[]{:S(2)}) collective-permute-start(bf16[384,128]{1,0:T(8,128)(2,1)S(1)} %get-tuple-element.43), channel_id=1, source_target_pairs={{0,130},{128,0},{2,128},{130,2},{1,131},{129,1},{3,129},{131,3},{4... | collective-permute-start | bytes 294920 | tf_op jit(solution)/shard_map/ppermute | solution.py:390
  15.4 10.1 %collective-permute-start.8 = (bf16[80,1024]{1,0:T(8,128)(2,1)S(1)}, bf16[80,1024]{1,0:T(8,128)(2,1)S(1)}, u32[]{:S(2)}, u32[]{:S(2)}) collective-permute-start(bf16[80,1024]{1,0:T(8,128)(2,1)S(1)} %get-tuple-element.44.qx.refs_0_), channel_id=1, source_target_pairs={{0,8},{4,12},{8,0},{12,4},{1,9},{5,13},{9,1},{13,5},{2,10},{6,14},... | collective-permute-start | bytes 491528 | tf_op jit(solution)/shard_map/ppermute | solution.py:386
  17.4 9.1 %collective-permute-start.7 = (bf16[80,1024]{1,0:T(8,128)(2,1)S(1)}, bf16[80,1024]{1,0:T(8,128)(2,1)S(1)}, u32[]{:S(2)}, u32[]{:S(2)}) collective-permute-start(bf16[80,1024]{1,0:T(8,128)(2,1)S(1)} %get-tuple-element.44.qx.refs_0_), channel_id=1, source_target_pairs={{0,12},{4,0},{8,4},{12,8},{1,13},{5,1},{9,5},{13,9},{2,14},{6,2},{... | collective-permute-start | bytes 491528 | tf_op jit(solution)/shard_map/ppermute | solution.py:386
  18.3 8.2 %collective-permute-start.6 = (bf16[80,1024]{1,0:T(8,128)(2,1)S(1)}, bf16[80,1024]{1,0:T(8,128)(2,1)S(1)}, u32[]{:S(2)}, u32[]{:S(2)}) collective-permute-start(bf16[80,1024]{1,0:T(8,128)(2,1)S(1)} %get-tuple-element.44.qx.refs_0_), channel_id=1, source_target_pairs={{0,4},{4,8},{8,12},{12,0},{1,5},{5,9},{9,13},{13,1},{2,6},{6,10},{... | collective-permute-start | bytes 491528 | tf_op jit(solution)/shard_map/ppermute | solution.py:386
  18.9 9.7 %collective-permute-start.5 = (bf16[1024,128]{1,0:T(8,128)(2,1)S(1)}, bf16[1024,128]{1,0:T(8,128)(2,1)S(1)}, u32[]{:S(2)}, u32[]{:S(2)}) collective-permute-start(bf16[1024,128]{1,0:T(8,128)(2,1)S(1)} %get-tuple-element.45.kv.refs_2_.refs_1_.refs_4_), channel_id=1, source_target_pairs={{0,112},{16,0},{32,16},{48,32},{64,48},{80,64},{96,80},{112,96},{1... | collective-permute-start | bytes 786440 | tf_op jit(solution)/shard_map/ppermute | solution.py:386
  24.5 7.1 %collective-permute-start.4 = (bf16[1024,128]{1,0:T(8,128)(2,1)S(1)}, bf16[1024,128]{1,0:T(8,128)(2,1)S(1)}, u32[]{:S(2)}, u32[]{:S(2)}) collective-permute-start(bf16[1024,128]{1,0:T(8,128)(2,1)S(1)} %get-tuple-element.45.kv.refs_2_.refs_1_.refs_4_), channel_id=1, source_target_pairs={{0,16},{16,32},{32,48},{48,64},{64,80},{80,96},{96,112},{112,0},{1... | collective-permute-start | bytes 786440 | tf_op jit(solution)/shard_map/ppermute | solution.py:386
  31.6 8.2 %collective-permute-start.9 = (bf16[1024,128]{1,0:T(8,128)(2,1)S(1)}, bf16[1024,128]{1,0:T(8,128)(2,1)S(1)}, u32[]{:S(2)}, u32[]{:S(2)}) collective-permute-start(bf16[1024,128]{1,0:T(8,128)(2,1)S(1)} %collective-permute-done.4.up.refs_5_.refs_2_), channel_id=1, source_target_pairs={{0,16},{16,32},{32,48},{48,64},{64,80},{80,96},{96,112},{112,0},{1... | collective-permute-start | bytes 786440 | tf_op jit(solution)/shard_map/ppermute | solution.py:386
  31.6 8.2 %collective-permute-start.10 = (bf16[1024,128]{1,0:T(8,128)(2,1)S(1)}, bf16[1024,128]{1,0:T(8,128)(2,1)S(1)}, u32[]{:S(2)}, u32[]{:S(2)}) collective-permute-start(bf16[1024,128]{1,0:T(8,128)(2,1)S(1)} %collective-permute-done.5.down.refs_6_.refs_3_), channel_id=1, source_target_pairs={{0,112},{16,0},{32,16},{48,32},{64,48},{80,64},{96,80},{112,96},{1... | collective-permute-start | bytes 786440 | tf_op jit(solution)/shard_map/ppermute | solution.py:386
  39.8 8.2 %collective-permute-start.11 = (bf16[1024,128]{1,0:T(8,128)(2,1)S(1)}, bf16[1024,128]{1,0:T(8,128)(2,1)S(1)}, u32[]{:S(2)}, u32[]{:S(2)}) collective-permute-start(bf16[1024,128]{1,0:T(8,128)(2,1)S(1)} %collective-permute-done.9.refs_3_.refs_7_.refs_4_), channel_id=1, source_target_pairs={{0,16},{16,32},{32,48},{48,64},{64,80},{80,96},{96,112},{112,0},{1... | collective-permute-start | bytes 786440 | tf_op jit(solution)/shard_map/ppermute | solution.py:386
  39.9 8.2 %collective-permute-start.12 = (bf16[1024,128]{1,0:T(8,128)(2,1)S(1)}, bf16[1024,128]{1,0:T(8,128)(2,1)S(1)}, u32[]{:S(2)}, u32[]{:S(2)}) collective-permute-start(bf16[1024,128]{1,0:T(8,128)(2,1)S(1)} %collective-permute-done.10.refs_4_.refs_8_.refs_5_), channel_id=1, source_target_pairs={{0,112},{16,0},{32,16},{48,32},{64,48},{80,64},{96,80},{112,96},{1... | collective-permute-start | bytes 786440 | tf_op jit(solution)/shard_map/ppermute | solution.py:386
  48.1 6.5 %collective-permute-start.13 = (bf16[1024,128]{1,0:T(8,128)(2,1)S(1)}, bf16[1024,128]{1,0:T(8,128)(2,1)S(1)}, u32[]{:S(2)}, u32[]{:S(2)}) collective-permute-start(bf16[1024,128]{1,0:T(8,128)(2,1)S(1)} %collective-permute-done.11.refs_3_.refs_9_.refs_6_), channel_id=1, source_target_pairs={{0,16},{16,32},{32,48},{48,64},{64,80},{80,96},{96,112},{112,0},{1... | collective-permute-start | bytes 786440 | tf_op jit(solution)/shard_map/ppermute | solution.py:386
  144.8 30.7 %collective-permute-start.14 = (bf16[80,1024]{1,0:T(8,128)(2,1)S(1)}, bf16[80,1024]{1,0:T(8,128)(2,1)S(1)}, u32[]{:S(2)}, u32[]{:S(2)}) collective-permute-start(bf16[80,1024]{1,0:T(8,128)(2,1)S(1)} %get-tuple-element.57), channel_id=1, source_target_pairs={{0,12},{4,0},{8,4},{12,8},{1,13},{5,1},{9,5},{13,9},{2,14},{6,2},{... | collective-permute-start | bytes 491528 | tf_op jit(solution)/shard_map/ppermute | solution.py:386
  147.0 28.6 %collective-permute-start.15 = (bf16[80,1024]{1,0:T(8,128)(2,1)S(1)}, bf16[80,1024]{1,0:T(8,128)(2,1)S(1)}, u32[]{:S(2)}, u32[]{:S(2)}) collective-permute-start(bf16[80,1024]{1,0:T(8,128)(2,1)S(1)} %get-tuple-element.58), channel_id=1, source_target_pairs={{0,4},{4,8},{8,12},{12,0},{1,5},{5,9},{9,13},{13,1},{2,6},{6,10},{... | collective-permute-start | bytes 491528 | tf_op jit(solution)/shard_map/ppermute | solution.py:386
  147.0 28.6 %collective-permute-start.16 = (bf16[80,1024]{1,0:T(8,128)(2,1)S(1)}, bf16[80,1024]{1,0:T(8,128)(2,1)S(1)}, u32[]{:S(2)}, u32[]{:S(2)}) collective-permute-start(bf16[80,1024]{1,0:T(8,128)(2,1)S(1)} %get-tuple-element.59), channel_id=1, source_target_pairs={{0,8},{4,12},{8,0},{12,4},{1,9},{5,13},{9,1},{13,5},{2,10},{6,14},... | collective-permute-start | bytes 491528 | tf_op jit(solution)/shard_map/ppermute | solution.py:386
  175.7 11.6 %collective-permute-start.17 = (bf16[128,128]{1,0:T(8,128)(2,1)S(1)}, bf16[128,128]{1,0:T(8,128)(2,1)S(1)}, u32[]{:S(2)}, u32[]{:S(2)}) collective-permute-start(bf16[128,128]{1,0:T(8,128)(2,1)S(1)} %get-tuple-element.60), channel_id=1, source_target_pairs={{0,130},{128,0},{2,128},{130,2},{1,131},{129,1},{3,129},{131,3},{4... | collective-permute-start | bytes 98312 | tf_op jit(solution)/shard_map/ppermute | solution.py:390
  176.5 10.8 %collective-permute-start.18 = (bf16[128,128]{1,0:T(8,128)(2,1)S(1)}, bf16[128,128]{1,0:T(8,128)(2,1)S(1)}, u32[]{:S(2)}, u32[]{:S(2)}) collective-permute-start(bf16[128,128]{1,0:T(8,128)(2,1)S(1)} %get-tuple-element.61), channel_id=1, source_target_pairs={{0,2},{128,130},{2,0},{130,128},{1,3},{129,131},{3,1},{131,129},{4... | collective-permute-start | bytes 98312 | tf_op jit(solution)/shard_map/ppermute | solution.py:390
  177.2 10.2 %collective-permute-start.19 = (bf16[128,128]{1,0:T(8,128)(2,1)S(1)}, bf16[128,128]{1,0:T(8,128)(2,1)S(1)}, u32[]{:S(2)}, u32[]{:S(2)}) collective-permute-start(bf16[128,128]{1,0:T(8,128)(2,1)S(1)} %get-tuple-element.62), channel_id=1, source_target_pairs={{0,128},{128,2},{2,130},{130,0},{1,129},{129,3},{3,131},{131,1},{4... | collective-permute-start | bytes 98312 | tf_op jit(solution)/shard_map/ppermute | solution.py:390
  178.0 16.9 %copy-start = (bf16[1024,2048]{1,0:T(8,128)(2,1)S(1)}, bf16[1024,2048]{1,0:T(8,128)(2,1)}, u32[]{:S(2)}) copy-start(bf16[1024,2048]{1,0:T(8,128)(2,1)} %w_expand.1) | copy-start | bytes 12582916
  187.3 7.5 %copy-start.2 = (bf16[512,1024]{1,0:T(8,128)(2,1)S(1)}, bf16[512,1024]{1,0:T(8,128)(2,1)}, u32[]{:S(2)}) copy-start(bf16[512,1024]{1,0:T(8,128)(2,1)} %w_out.1) | copy-start | bytes 3145732
  187.3 7.5 %copy-start.3 = (bf16[128,1024]{1,0:T(8,128)(2,1)S(1)}, bf16[128,1024]{1,0:T(8,128)(2,1)}, u32[]{:S(2)}) copy-start(bf16[128,1024]{1,0:T(8,128)(2,1)} %frames.1) | copy-start | bytes 786436
  187.3 7.5 %copy-start.5 = (f32[1024]{0:T(1024)S(1)}, f32[1024]{0:T(1024)}, u32[]{:S(2)}) copy-start(f32[1024]{0:T(1024)} %param.18) | copy-start | bytes 12292
  187.4 7.4 %collective-permute-start.20 = (bf16[256,128]{1,0:T(8,128)(2,1)S(1)}, bf16[256,128]{1,0:T(8,128)(2,1)S(1)}, u32[]{:S(2)}, u32[]{:S(2)}) collective-permute-start(bf16[256,128]{1,0:T(8,128)(2,1)S(1)} %shard_map.131), channel_id=1, source_target_pairs={{0,1},{1,0},{2,3},{3,2},{4,5},{5,4},{6,7},{7,6},{8,9},{9,8},{10,11... | collective-permute-start | bytes 196616 | tf_op jit(solution)/shard_map/ppermute | solution.py:386
  194.8 6.2 %copy-start.4 = (f32[31,1024]{1,0:T(8,128)S(1)}, f32[31,1024]{1,0:T(8,128)}, u32[]{:S(2)}) copy-start(f32[31,1024]{1,0:T(8,128)} %taps.3) | copy-start | bytes 380932
  196.7 6.7 %collective-permute-start.22 = (bf16[16,1024]{1,0:T(8,128)(2,1)S(1)}, bf16[16,1024]{1,0:T(8,128)(2,1)S(1)}, u32[]{:S(2)}, u32[]{:S(2)}) collective-permute-start(bf16[16,1024]{1,0:T(8,128)(2,1)S(1)} %get-tuple-element.67), channel_id=1, source_target_pairs={{2,1},{4,3},{6,5},{8,7},{10,9},{12,11},{14,13},{16,15},{18,17},{20... | collective-permute-start | bytes 98312 | tf_op jit(solution)/shard_map/ppermute | solution.py:460
  201.1 2.5 %copy-start.1 = (bf16[1024,1024]{1,0:T(8,128)(2,1)S(1)}, bf16[1024,1024]{1,0:T(8,128)(2,1)}, u32[]{:S(2)}) copy-start(bf16[1024,1024]{1,0:T(8,128)(2,1)} %w_project.1) | copy-start | bytes 6291460
  201.1 2.5 %copy-start.6 = (f32[1024]{0:T(1024)S(1)}, f32[1024]{0:T(1024)}, u32[]{:S(2)}) copy-start(f32[1024]{0:T(1024)} %param.21) | copy-start | bytes 12292
  201.1 2.5 %copy-start.7 = (f32[1024]{0:T(1024)S(1)}, f32[1024]{0:T(1024)}, u32[]{:S(2)}) copy-start(f32[1024]{0:T(1024)} %param.22) | copy-start | bytes 12292
  202.3 1.3 collective-permute-start.21
